TPU v7x, 32 devices: a whole 2x2x4 slice. The times are simulated.
32 devices in a mesh: dp: 16 (over z, y, x), seq: 2 (over core).
Axes of the slice: x: 2, y: 2, z: 4, core: 2. Of those that a mesh axis runs over, the one named last changes fastest.
Arguments:
- tokens: bfloat16 [2, 32, 512, 512], P(None, 'dp', 'seq'), may hold values from -6 to 6
- cotangent: bfloat16 [2, 32, 512, 512], P(None, 'dp', 'seq'), may hold values from -6 to 6
- segments: int32 [2, 32, 512], P(None, 'dp', 'seq'), may hold values from 0 to 3, as said below
- pad_mask: int32 [2, 32, 512], P(None, 'dp', 'seq'), may hold values from 0 to 1, as said below
- row_counts: int32 [2, 16], P(None, 'dp'), may hold values from 1 to 2, as said below
- attend_gain: float32 [512], replicated, may hold values from 0.5 to 1.5
- w_query: bfloat16 [512, 512], replicated, may hold values from -0.125 to 0.125
- w_key: bfloat16 [512, 512], replicated, may hold values from -0.125 to 0.125
- w_value: bfloat16 [512, 512], replicated, may hold values from -0.25 to 0.25
- w_out: bfloat16 [512, 512], replicated, may hold values from -0.75 to 0.75
- forward_gain: float32 [512], replicated, may hold values from 0.5 to 1.5
- w_in: bfloat16 [512, 2048], replicated, may hold values from -0.25 to 0.25
- w_down: bfloat16 [2048, 512], replicated, may hold values from -0.125 to 0.125
- position_bias_table: float32 [32, 8], replicated, may hold values from -4 to 4
Outputs:
- output: bfloat16 [2, 32, 512, 512], P(None, 'dp', 'seq')
- gradient_input: bfloat16 [2, 32, 512, 512], P(None, 'dp', 'seq')
- grad_attend: float32 [512], replicated
- grad_query: float32 [512, 512], replicated
- grad_key: float32 [512, 512], replicated
- grad_value: float32 [512, 512], replicated
- grad_out: float32 [512, 512], replicated
- grad_forward: float32 [512], replicated
- grad_in: float32 [512, 2048], replicated
- grad_down: float32 [2048, 512], replicated
- grad_table: float32 [32, 8], replicated
Inputs may be any that keep to these rules, and one draw needn't show every extreme that they name: Rows of data group g with slot number row_counts[m, g] or more in micro-batch m are unused; in every draw some group has 2 live rows and some has one. `segments`: each row is cut into items of 128, 256 or 512 tokens that start on quarters of the row, numbered from 0 at the row's start; in each micro-batch every data group has a live row that is one item of 512 tokens. `pad_mask`: within an item the real tokens come first and are more than seven eighths of it.
All inputs are finite; a program needn't handle non-finite values.
Results may differ from a plain program's by a relative error of at most 0.014.
Values may be sent and summed in bfloat16 or wider, within the bound.
No kernel may reach another device: no remote copies, remote signals or barrier semaphores. Data moves between devices by JAX's collectives and lax.ppermute only.
A program may use at most 192 MiB of HBM per device.

v0:
```python
import functools
import math

import jax
import jax.numpy as jnp
from jax import lax
from jax.experimental import pallas as pl
from jax.experimental.pallas import tpu as pltpu
from jax.sharding import PartitionSpec as P

EPSILON = 1e-06
MASKED = -1000000000.0
LIMITS = (12, 16, 23, 32, 46, 64, 91)
BF = jnp.bfloat16
F32 = jnp.float32
TILE = 128
LEVELS = 4
SPLIT = 2
SMALL = 32
PARTS = 2
FREE = ("pick_rest", "attend_forward", "feed_first", "feed_third")
ORDERS = ([(0, 2), (1, 0), (2, 1)], [(1, 0), (2, 1), (0, 2)])
VMEM = (16, 15, 12, 14, 12, 10, 10, 14)


def whole():
    return pl.BlockSpec(memory_space=pltpu.VMEM)


def hbm():
    return pl.BlockSpec(memory_space=pl.ANY)


def far():
    return pl.BlockSpec(memory_space=pltpu.HBM)


def smem():
    return pl.BlockSpec(memory_space=pltpu.SMEM)


class Order:
    def __init__(self):
        self.token = None

    def call(self, kernel, name, micros, inputs, in_specs, out_shape, grid=1, out_specs=None, scratch=(), vmem=8, aliases=None, who=None):
        count, results = len(inputs), len(out_shape)
        extra = () if self.token is None or name in FREE else (self.token,)

        skip = count + len(extra)

        def body(*refs):
            token = refs[skip + results]
            token[...] = jnp.zeros_like(token)
            first = () if who is None else (who(),)
            kernel(*first, *refs[:count], *refs[skip : skip + results], *refs[skip + results + 1 :])

        *outs, self.token = pl.pallas_call(
            body,
            grid=(grid,),
            in_specs=list(in_specs) + [whole()] * len(extra),
            out_specs=list(out_specs or [whole() for _ in out_shape]) + [whole()],
            out_shape=(*out_shape, jax.ShapeDtypeStruct((8, TILE), F32)),
            scratch_shapes=list(scratch),
            input_output_aliases=aliases or {},
            compiler_params=pltpu.CompilerParams(vmem_limit_bytes=vmem * 1024 * 1024),
            cost_estimate=pl.CostEstimate(
                flops=int(micros * 1e9), bytes_accessed=int(micros * 1e6), transcendentals=0
            ),
            name=name,
        )(*inputs, *extra)
        return outs


def dot(a, b, contract=((1,), (0,))):
    return lax.dot_general(a, b, (contract, ((), ())), preferred_element_type=F32)


def dot_nt(a, b):
    return dot(a, b, ((1,), (1,)))


def dot_tn(a, b):
    return dot(a, b, ((0,), (0,)))


def bucket_of(relative, half_count):
    distance = jnp.abs(relative)
    far = jnp.full(relative.shape, 8, jnp.int32)
    for bound in LIMITS:
        far = far + (distance >= bound).astype(jnp.int32)
    near_or_far = jnp.where(distance < 8, distance, far)
    return near_or_far + jnp.where(relative > 0, half_count, 0)


def diagonal_buckets(length, half_count):
    lane = lax.broadcasted_iota(jnp.int32, (8, 2 * length), 1)
    relative = lane - (length - TILE)
    relative = jnp.where(lane < 2 * length - TILE, relative, relative - 2 * length)
    return bucket_of(relative, half_count)


def wide(column, width):
    return jnp.concatenate([column] * (width // TILE), axis=1)


def put_block(keep, send, who, block, blocks, value):
    count = value.shape[0] >> LEVELS
    places = 1 << LEVELS
    for core in range(2):

        @pl.when(who[0] == core)
        def _():
            for k in range(places):
                place = jnp.bitwise_xor(k % (places // 2), who[1 + 2 * k // places])
                start = pl.multiple_of((place * blocks + block) * count, count)
                ref = keep if 2 * k // places == core else send
                ref[pl.ds(start, count), :] = value[k * count : (k + 1) * count].astype(ref.dtype)


def half_of(ref, i, half):
    return ref[pl.ds(pl.multiple_of(i * half, half), half), :]


def fill_row(row_ref, own_ref, got_ref, m, c, half):
    row_ref[m, pl.ds(pl.multiple_of(c * half, half), half), :] = own_ref[m]
    row_ref[m, pl.ds(pl.multiple_of((1 - c) * half, half), half), :] = got_ref[m]
    return row_ref[m]


def join(own, got, c):
    return jnp.where(c == 0, jnp.concatenate([own, got], 1), jnp.concatenate([got, own], 1))


def fetches(sources, targets, sems):
    return [pltpu.make_async_copy(a, b, sems.at[i]) for i, (a, b) in enumerate(zip(sources, targets))]


def feed_weights(w_in, w_down, chunk, width):
    start = pl.multiple_of(chunk * width, width)
    return w_in.at[:, pl.ds(start, width)], w_down.at[pl.ds(start, width), :]


def pick_kernel(who, tok, seg, pad, tok_send, marks_own, marks_send, sems):
    c = who[0]
    rows = tok.shape[0]
    copies = [pltpu.make_async_copy(tok.at[m, 1 - c], tok_send.at[m], sems.at[m]) for m in range(rows)]
    for copy in copies:
        copy.start()
    for kind, marks in enumerate((seg, pad)):
        for m in range(rows):
            first, second = marks[m, pl.ds(0, 1)], marks[m, pl.ds(1, 1)]
            marks_own[kind, pl.ds(m, 1)] = jnp.where(c == 0, first, second)
            marks_send[kind, pl.ds(m, 1)] = jnp.where(c == 0, second, first)
    for copy in copies:
        copy.wait()


def pick_rest_kernel(who, tok, cot, tok_own, cot_own, cot_send, sems):
    c = who[0]
    copies = []
    for m in range(tok.shape[0]):
        for source, slot, target in ((tok, c, tok_own), (cot, 1 - c, cot_send), (cot, c, cot_own)):
            copies.append(pltpu.make_async_copy(source.at[m, slot], target.at[m], sems.at[len(copies)]))
    for copy in copies:
        copy.start()
    for copy in copies:
        copy.wait()


def place_kernel(who, *refs):
    c = who[0]
    count = (len(refs) - 1) // 3
    sems = refs[-1]
    copies = []
    for i in range(count):
        own, got, out = refs[2 * i], refs[2 * i + 1], refs[2 * count + i]
        for m in range(own.shape[0]):
            for source, slot in ((own, c), (got, 1 - c)):
                copies.append(pltpu.make_async_copy(source.at[m], out.at[m, slot], sems.at[len(copies)]))
    for copy in copies:
        copy.start()
    for copy in copies:
        copy.wait()


def forward_kernel(
    who, counts, own, got, marks, marks_got, table, gain, fgain, wq_far, wk_far, wv_far, wo_far,
    x_out, normed_out, q_out, k_out, v_out, e_out, inv_out, att_out, kept_out, middle_out, second_out,
    segq, segk, diag, wq, wk, wv, wo, sems,
):
    c = who[0]
    pair = pl.program_id(0)
    rows, half = own.shape[0], own.shape[1]
    length = 2 * half
    pairs = wq.shape[1] // TILE
    bucket_count = table.shape[0]
    copies = fetches((wq_far, wk_far, wv_far, wo_far), (wq, wk, wv, wo), sems)

    @pl.when(pair == 0)
    def _():
        for copy in copies:
            copy.start()
        buckets = diagonal_buckets(length, bucket_count // 2)
        strip = jnp.zeros(buckets.shape, F32)
        for b in range(bucket_count):
            strip = jnp.where(buckets == b, table[b], strip)
        for h in range(strip.shape[0]):
            diag[h] = strip[h : h + 1]
        for m in range(rows):
            x = fill_row(x_out, own, got, m, c, half).astype(F32)
            r = lax.rsqrt(jnp.mean(x * x, -1, keepdims=True) + EPSILON)
            normed = (x * r * gain[...]).astype(BF)
            normed_out[m] = normed
            if m == 0:
                for copy in copies:
                    copy.wait()
            for w, out in ((wq, q_out), (wk, k_out), (wv, v_out)):
                projected = dot(normed, w[...]).astype(BF)
                for p in range(pairs):
                    out[m, p] = projected[:, p * TILE : (p + 1) * TILE]
            seg = join(marks[0, pl.ds(m, 1)], marks_got[0, pl.ds(m, 1)], c)
            pad = join(marks[1, pl.ds(m, 1)], marks_got[1, pl.ds(m, 1)], c)
            kept = (pad > 0) & (counts[m] > c)
            item = lax.broadcasted_iota(jnp.int32, (TILE, length), 0)
            same = item == seg
            segq[m] = jnp.where(same, 1.0, 0.0).T.astype(BF)
            segk[m] = jnp.where(same & kept, 0.0, MASKED).T.astype(BF)
            kept_out[m] = jnp.broadcast_to(jnp.where(kept, 1.0, 0.0), (TILE, length)).T

    lane = lax.broadcasted_iota(jnp.int32, (length, TILE), 1)
    for head in range(2):
        mine = (lane < TILE // 2) if head == 0 else (lane >= TILE // 2)
        line = jnp.broadcast_to(diag[2 * pair + head], (TILE, 2 * length))
        strip = pltpu.roll(line, 0, 1, stride=1, stride_axis=0)
        bias = jnp.concatenate(
            [strip[:, length - (i + 1) * TILE : 2 * length - (i + 1) * TILE] for i in range(length // TILE)], 0
        )
        for m in range(rows):
            query = jnp.concatenate([q_out[m, pair], segq[m]], 1)
            key = jnp.concatenate([jnp.where(mine, k_out[m, pair], 0), segk[m]], 1)
            value = jnp.concatenate([jnp.where(mine, v_out[m, pair], 0), jnp.where(mine, 1.0, 0.0).astype(BF)], 1)
            scores = dot_nt(query, key) + bias
            e = jnp.exp(scores - jnp.max(scores, -1, keepdims=True)).astype(BF)
            e_out[m, 0, head] = e
            weighed = dot(e, value)
            if head == 0:
                att_acc = weighed
                inv_out[m, pair] = att_acc[:, TILE:]
                half_att = att_acc[:, :TILE]
                middle_out[m, :, :TILE] = half_att
            else:
                inv = 1.0 / (inv_out[m, pair] + weighed[:, TILE:])
                inv_out[m, pair] = inv
                att_out[m, pair] = ((middle_out[m, :, :TILE] + weighed[:, :TILE]) * inv).astype(BF)

    @pl.when(pair == pairs - 1)
    def _():
        for m in range(rows):
            attended = jnp.concatenate([att_out[m, p] for p in range(pairs)], 1)
            branch = dot(attended, wo[...])
            middle = x_out[m].astype(F32) + wide(kept_out[m], branch.shape[1]) * branch
            middle_out[m] = middle
            r = lax.rsqrt(jnp.mean(middle * middle, -1, keepdims=True) + EPSILON)
            second_out[m] = (middle * r * fgain[...]).astype(BF)


def gelu_parts(u):
    z = jnp.abs(u) * (0.5**0.5)
    t = 1.0 / (1.0 + 0.3275911 * z)
    bell = jnp.exp(u * u * -0.5)
    poly = ((((1.061405429 * t - 1.453152027) * t + 1.421413741) * t - 0.284496736) * t + 0.254829592) * t
    tail = 0.5 * poly * bell
    upper = jnp.where(u >= 0, 1.0 - tail, tail)
    return upper, u * bell * ((2.0 * math.pi) ** -0.5)


def feed_chunk(second, fg, w_in, w_down, acc, sg):
    down = into = None
    for m in range(second.shape[0]):
        u = dot(second[m], w_in[...])
        upper, slope = gelu_parts(u)
        active = (u * upper).astype(BF)
        acc[m] += dot(active, w_down[...])
        up = (dot_nt(fg[m], w_down[...]) * (upper + slope)).astype(BF)
        sg[m] += dot_nt(up, w_in[...])
        down_now, into_now = dot_tn(active, fg[m]), dot_tn(second[m], up)
        down = down_now if m == 0 else down + down_now
        into = into_now if m == 0 else into + into_now
    return down, into


def tall(ref):
    return jnp.concatenate([ref[m] for m in range(ref.shape[0])], 0)


def feed_first_kernel(
    who, own, got, kept, second, w_in_far, w_down_far,
    g_out, fg_out, acc_out, sg_out, keep, send,
    w_ins, w_downs, sems,
    *, steps,
):
    step = pl.program_id(0)
    rows, half, width = own.shape
    copies = [
        fetches(feed_weights(w_in_far, w_down_far, i, width), (w_ins.at[i], w_downs.at[i]), sems.at[i])
        for i in range(steps)
    ]

    @pl.when(step == 0)
    def _():
        for copy in sum(copies, []):
            copy.start()
        for m in range(rows):
            g = fill_row(g_out, own, got, m, who[0], half)
            fg_out[m] = (g.astype(F32) * wide(kept[m], g.shape[1])).astype(BF)
        acc_out[...] = jnp.zeros_like(acc_out)
        sg_out[...] = jnp.zeros_like(sg_out)

    for i in range(steps):

        @pl.when(step == i)
        def _():
            for copy in copies[i]:
                copy.wait()

    down, into = feed_chunk(second, fg_out, w_ins.at[step], w_downs.at[step], acc_out, sg_out)
    put_block(keep, send, who, step, 2 * steps, down)
    put_block(keep, send, who, steps + step, 2 * steps, into)


def feed_third_kernel(
    chunk, who, g, fg, acc_in, sg_in, kept, middle, second, att, fgain, wo_far, w_in_far, w_down_far,
    acc, sg, keep_out, send_out, mg_out, back_out, gf_out, down_out, in_out, o_out,
    half_rows, w_in, w_down, wo, sems,
):
    c = who[0]
    rows, length, width = g.shape
    half = length // 2
    pairs = width // TILE
    copies = fetches((*feed_weights(w_in_far, w_down_far, chunk, width), wo_far), (w_in, w_down, wo), sems)
    for copy in copies:
        copy.start()
    for copy in copies:
        copy.wait()
    down, into = feed_chunk(second, fg, w_in, w_down, acc, sg)
    down_out[...] = down.astype(BF)
    in_out[...] = into.astype(BF)
    gf = jnp.zeros(gf_out.shape, F32)
    for m in range(rows):
        mid = middle[m]
        held = wide(kept[m], width)
        half_rows[...] = mid + held * acc[m]
        keep_out[m] = half_of(half_rows, c, half).astype(BF)
        send_out[m] = half_of(half_rows, 1 - c, half).astype(BF)
        r = lax.rsqrt(jnp.mean(mid * mid, -1, keepdims=True) + EPSILON)
        later = sg[m]
        across = later * mid
        gf = gf + jnp.sum(across * r, 0, keepdims=True)
        inner = jnp.mean(across * fgain[...], -1, keepdims=True)
        mg = g[m].astype(F32) + r * (later * fgain[...]) - mid * (r * r * r * inner)
        mg_out[m] = mg
        branch = (held * mg).astype(BF)
        back = dot_nt(branch, wo[...]).astype(BF)
        attended = jnp.concatenate([att[m, p] for p in range(pairs)], 1)
        for p in range(pairs):
            back_out[m, p] = back[:, p * TILE : (p + 1) * TILE]
        out_now = dot_tn(attended, branch)
        go = out_now if m == 0 else go + out_now
    gf_out[...] = gf
    o_out[...] = go.astype(BF)


def backward_kernel(
    e_in, q, k, v, inv, att, grad_att,
    dq_out, dk_out, dv_out, diag_out,
    strip,
    *, base,
):
    step = pl.program_id(0)
    pair = step + base
    rows, length = q.shape[0], q.shape[2]
    lane = lax.broadcasted_iota(jnp.int32, (length, TILE), 1)
    low = lane < TILE // 2
    strip[...] = jnp.zeros_like(strip)
    for m in range(rows):
        got = grad_att[m, pair].astype(F32)
        inverse = inv[m, pair]
        scaled = (got * inverse).astype(BF)
        weighed = got * inverse * att[m, pair].astype(F32)
        extra = jnp.zeros((length, TILE), F32)
        for head in range(2):
            mine = low if head == 0 else jnp.logical_not(low)
            centre = -jnp.sum(jnp.where(mine, weighed, 0.0), -1, keepdims=True)
            rough = centre.astype(BF).astype(F32)
            extra = jnp.where(lane == 2 * head, rough, extra)
            extra = jnp.where(lane == 2 * head + 1, centre - rough, extra)
        left = jnp.concatenate([scaled, extra.astype(BF)], 1)
        dq = dk = dv = None
        for head in range(2):
            mine = low if head == 0 else jnp.logical_not(low)
            ones = jnp.where((lane == 2 * head) | (lane == 2 * head + 1), 1.0, 0.0).astype(BF)
            right = jnp.concatenate([jnp.where(mine, v[m, pair], 0), ones], 1)
            e = e_in[m, 0, head]
            ds = e.astype(F32) * dot_nt(left, right)
            for i in range(length // TILE):
                start = length - (i + 1) * TILE
                strip[head, :, start : start + length] += ds[i * TILE : (i + 1) * TILE]
            ds = ds.astype(BF)
            dq_now = dot(ds, jnp.where(mine, k[m, pair], 0))
            dk_now = dot_tn(ds, jnp.where(mine, q[m, pair], 0))
            dv_now = dot_tn(e, jnp.where(mine, scaled, 0))
            dq = dq_now if dq is None else dq + dq_now
            dk = dk_now if dk is None else dk + dk_now
            dv = dv_now if dv is None else dv + dv_now
        dq_out[m, step] = dq.astype(BF)
        dk_out[m, step] = dk.astype(BF)
        dv_out[m, step] = dv.astype(BF)
    lanes = strip.shape[2]
    for head in range(2):
        total = strip[head]
        count = TILE
        while count > 1:
            count //= 2
            total = total[:count] + pltpu.roll(total[count:], lanes - count, 1)
        diag_out[2 * step + head] = total


def joined(grads, m):
    return jnp.concatenate([grad[m, p] for grad in grads for p in range(grad.shape[1])], 1)


def weight_kernel(parts, bucket_count, *refs):
    who, normed = refs[:2]
    dq, dk, dv, diags = (refs[2 + i * parts : 2 + (i + 1) * parts] for i in range(4))
    gf, *blocks = refs[2 + 4 * parts : 6 + 4 * parts]
    wq_far, wk_far, wv_far, gain, keep, send, small_out, wq, wk, wv, sems = refs[6 + 4 * parts :]
    rows, length, width = normed.shape
    copies = fetches((wq_far, wk_far, wv_far), (wq, wk, wv), sems)
    for copy in copies:
        copy.start()
    n = tall(normed)
    summed = jnp.zeros((width, 1), F32)
    for place, (grads, weight) in enumerate(((dq, wq), (dk, wk), (dv, wv))):
        value = dot_tn(n, jnp.concatenate([joined(grads, m) for m in range(rows)], 0))
        copies[place].wait()
        summed = summed + jnp.sum(value * weight[...].astype(F32), -1, keepdims=True)
        put_block(keep, send, who, 3 + place, 6, value)
    for place, ready in enumerate(blocks):
        put_block(keep, send, who, place, 6, ready[...])
    ga = jnp.broadcast_to(summed, (width, TILE)).T[:1] / gain[...]
    lines = jnp.concatenate([diag[h] for diag in diags for h in range(diag.shape[0])], 0)
    buckets = diagonal_buckets(length, bucket_count // 2)
    lane = lax.broadcasted_iota(jnp.int32, (8, width), 1)
    table = jnp.zeros((8, width), F32)
    for b in range(bucket_count):
        total = jnp.sum(jnp.where(buckets == b, lines, 0.0), -1, keepdims=True)
        table = jnp.where(lane == b, total, table)
    small = jnp.concatenate([ga, gf[...], jnp.zeros((6, width), F32), table], 0)
    rough = small.astype(BF)
    small = jnp.concatenate([rough, (small - rough.astype(F32)).astype(BF)], 0)
    small_out[...] = small
    send[send.shape[0] - small.shape[0] :, :] = small


def input_kernel(parts, *refs):
    who, x, mg = refs[:3]
    dq, dk, dv = (refs[3 + i * parts : 3 + (i + 1) * parts] for i in range(3))
    wq_far, wk_far, wv_far, gain, keep_out, send_out, half_rows, wq, wk, wv, sems = refs[3 + 3 * parts :]
    copies = fetches((wq_far, wk_far, wv_far), (wq, wk, wv), sems)
    for copy in copies:
        copy.start()
    c = who[0]
    rows, length, width = x.shape
    half = length // 2
    for m in range(rows):
        back = None
        for i, (grads, weight) in enumerate(((dq, wq), (dk, wk), (dv, wv))):
            if m == 0:
                copies[i].wait()
            now = dot_nt(joined(grads, m), weight[...])
            back = now if back is None else back + now
        xm = x[m].astype(F32)
        r = lax.rsqrt(jnp.mean(xm * xm, -1, keepdims=True) + EPSILON)
        grown = back * gain[...]
        inner = jnp.mean(grown * xm, -1, keepdims=True)
        half_rows[...] = mg[m] + r * grown - xm * (r * r * r * inner)
        keep_out[m] = half_of(half_rows, c, half).astype(BF)
        send_out[m] = half_of(half_rows, 1 - c, half).astype(BF)


def fill_block(target, i, blocks, who, own, got):
    places = 1 << LEVELS
    count = target.shape[0] >> LEVELS
    for k in range(places):
        core = 2 * k // places
        place = jnp.bitwise_xor(k % (places // 2), who[1 + core])
        start = pl.multiple_of((place * blocks + i) * count, count)
        mine = who[0] == core
        value = jnp.where(mine, own[pl.ds(start, count), :], got[pl.ds(start, count), :])
        target[k * count : (k + 1) * count, :] = value.astype(F32)


def feed_result_kernel(who, own, got, down_out, in_out, made, sems):
    width = own.shape[1]
    steps = made.shape[0] // 2
    copies = []
    for i in range(2 * steps):
        fill_block(made.at[i], i, 2 * steps, who, own, got)
        part = slice((i % steps) * width, (i % steps + 1) * width)
        target = down_out.at[part, :] if i < steps else in_out.at[:, part]
        copies.append(pltpu.make_async_copy(made.at[i], target, sems.at[i]))
        copies[-1].start()
    for copy in copies:
        copy.wait()


def rest_result_kernel(
    who, own, got, down_in, in_in, down_out, in_out, o_out, q_out, k_out, v_out, ga_out, gf_out, table_out, made, sems
):
    width = own.shape[1]
    last = slice(down_out.shape[0] - width, down_out.shape[0])
    targets = (down_out.at[last, :], in_out.at[:, last], o_out, q_out, k_out, v_out)
    copies = []
    for i, target in enumerate(targets):
        fill_block(made.at[i], i, 6, who, own, got)
        copies.append(pltpu.make_async_copy(made.at[i], target, sems.at[i]))
        copies[-1].start()
    tail = own.shape[0] - SMALL
    small = jnp.where(who[0] == 0, own[tail:, :].astype(F32), got[tail:, :].astype(F32))
    small = small[: SMALL // 2] + small[SMALL // 2 :]
    ga_out[...] = small[:1]
    gf_out[...] = small[1:2]
    table = jnp.concatenate([small[8:, :TILE], jnp.zeros((TILE - 8, TILE), F32)], 0).T
    table_out[...] = table[: table_out.shape[0], : table_out.shape[1]]
    for copy in copies:
        copy.wait()


def land_kernel(has_small, then, *refs):
    kind, after = then
    keep, got = refs[:2]
    refs = refs[2:]
    rows = keep.shape[0]
    if has_small:
        small, refs = refs[0], refs[1:]
    send = refs[0]
    if kind == "gather":
        send[:rows, :] = keep[...]
        send[rows : 2 * rows, :] = got[...]
        if has_small:
            send[2 * rows :, :] = small[...]
        return
    total = (keep[...].astype(F32) + got[:rows, :].astype(F32)).astype(BF)
    if after == "halve":
        refs[1][...] = total[: rows // 2]
        total = total[rows // 2 :]
    send[: total.shape[0], :] = total
    if has_small:
        half = SMALL // 2
        grown = (small[:half, :].astype(F32) + got[rows : rows + half, :].astype(F32)) + (
            small[half:, :].astype(F32) + got[rows + half :, :].astype(F32)
        )
        rough = grown.astype(BF)
        grown = jnp.concatenate([rough, (grown - rough.astype(F32)).astype(BF)], 0)
        refs[-1][...] = grown
        if after != "gather":
            send[total.shape[0] :, :] = grown
            if after != "halve":
                refs[1][...] = total


def swap_pairs(dp, bits):
    if bits is None:
        return [(i, i ^ 1) for i in range(2 * dp)]
    return [(i, i ^ (2 << bits[i % 2])) for i in range(2 * dp)]


class Piece:
    def __init__(self, calls, keep, send, small, order, rest, dp):
        self.calls, self.keep, self.send, self.small, self.dp = calls, keep, send, small, dp
        steps = [("halve", None)] + [("halve", bits) for bits in order]
        steps += [("exchange", (bit, bit)) for bit in rest]
        self.steps = steps + [("gather", bits) for bits in order[::-1]] + [("finish", None)]
        self.got = None
        self.fly()

    def fly(self):
        self.got = lax.ppermute(self.send, ("dp", "seq"), swap_pairs(self.dp, self.steps[0][1]))

    def land(self):
        kind, _ = self.steps.pop(0)
        after = self.steps[0][0]
        rows, width = self.keep.shape
        small = self.small is not None and (kind != "gather" or after == "finish")
        more = SMALL if small and after != "gather" else 0
        sds = lambda count: jax.ShapeDtypeStruct((count, width), BF)
        if kind == "gather":
            outs = [sds(2 * rows + more)]
        elif after == "halve":
            outs = [sds(rows // 2 + more), sds(rows // 2)]
        else:
            outs = [sds(rows + more)] + [sds(rows)] * (more > 0)
        if small and kind != "gather":
            outs.append(sds(SMALL))
        inputs = [self.keep, self.got] + [self.small] * small
        outs = self.calls.call(
            functools.partial(land_kernel, small, (kind, after)), "land", 0.5, inputs, [whole()] * len(inputs), outs
        )
        self.send = outs[0]
        if small and kind != "gather":
            self.small = outs[-1]
        split = kind != "gather" and (after == "halve" or more > 0)
        self.keep = outs[1] if split else outs[0]
        self.fly()
        return self

    def done(self):
        while len(self.steps) > 1:
            self.land()
        return self.send, self.got


def on_device(
    tokens, cotangent, segments, pad_mask, row_counts, attend_gain, w_query, w_key, w_value, w_out,
    forward_gain, w_in, w_down, position_bias_table,
):
    rows, slots, half, width = tokens.shape
    dp, seq = lax.axis_size("dp"), lax.axis_size("seq")
    bits = dp.bit_length() - 1
    assert seq == 2 and slots == 2 and dp == 1 << bits and bits >= 3
    length = seq * half
    inner = w_query.shape[1]
    ff = w_in.shape[1]
    bucket_count, heads = position_bias_table.shape
    pairs = inner // TILE
    assert heads == 2 * pairs == 8 and inner == width
    blocks = ff // width
    assert blocks == SPLIT + 2
    splits = (SPLIT, 2)
    orders = ORDERS
    rests = [[bit for bit in range(bits) if all(bit not in pair for pair in order)] for order in orders]

    def where_am_i(order):
        def who():
            here = lax.axis_index("dp")
            masks = []
            for core in range(2):
                mask = jnp.int32(0)
                for pair in order:
                    mask = 2 * mask + ((here >> pair[core]) & 1)
                masks.append(mask)
            return [lax.axis_index("seq"), *masks]

        return who

    who = [where_am_i(order) for order in orders]
    swap = lambda a: lax.ppermute(a, ("dp", "seq"), swap_pairs(dp, None))
    tokens, cotangent, w_query, w_key, w_value, w_out, w_in, w_down = (
        pltpu.with_memory_space_constraint(array, pltpu.HBM)
        for array in (tokens, cotangent, w_query, w_key, w_value, w_out, w_in, w_down)
    )
    table = jnp.broadcast_to(position_bias_table[:, :, None], (bucket_count, heads, 1))
    gain, fgain = attend_gain.reshape(1, width), forward_gain.reshape(1, width)
    sds = jax.ShapeDtypeStruct
    vm = pltpu.VMEM
    dma = pltpu.SemaphoreType.DMA
    paired = sds((rows, pairs, length, TILE), BF)
    wide_bf, wide_f32 = sds((rows, length, width), BF), sds((rows, length, width), F32)
    narrow, items = sds((rows, length, TILE), F32), sds((rows, length, TILE), BF)
    square, square_bf = sds((inner, width), F32), sds((inner, width), BF)
    row_half, marked = sds((rows, half, width), BF), sds((2, rows, half), jnp.int32)
    calls = Order()
    call = calls.call

    tok_send, marks_own, marks_send = call(
        pick_kernel, "pick", 1, (tokens, segments, pad_mask), [far(), whole(), whole()],
        (row_half, marked, marked), scratch=[dma((rows,))], who=who[0],
    )
    tok_got, marks_got = swap(tok_send), swap(marks_send)
    tok_own, cot_own, cot_send = call(
        pick_rest_kernel, "pick_rest", 1, (tokens, cotangent), [far(), far()],
        (row_half, row_half, row_half), scratch=[dma((3 * rows,))], who=who[0],
    )
    cot_got = swap(cot_send)
    e_shape = (rows, pairs, 2, length, length)
    x, normed, q, k, v, e, inv, att, kept, middle, second = call(
        forward_kernel, "attend_forward", 14,
        (
            row_counts.reshape(rows), tok_own, tok_got, marks_own, marks_got, table, gain, fgain,
            w_query, w_key, w_value, w_out,
        ),
        [smem()] + [whole()] * 7 + [far()] * 4,
        (
            wide_bf, wide_bf, paired, paired, paired, sds(e_shape, BF),
            sds((rows, pairs, length, TILE), F32), paired, narrow, wide_f32, wide_bf,
        ),
        grid=pairs,
        out_specs=[whole()] * 5 + [pl.BlockSpec((rows, 1, 2, length, length), lambda p: (0, p, 0, 0, 0))] + [whole()] * 5,
        scratch=[vm((rows, length, TILE), BF)] * 2 + [vm((heads, 1, 2 * length), F32)] + [vm((width, inner), BF)] * 4 + [dma((4,))],
        vmem=VMEM[0],
        who=who[0],
    )

    block = vm((width, width), BF)
    piece_halves = lambda count, more=0: (sds((count * width // 2, width), BF), sds((count * width // 2 + more, width), BF))
    first = blocks - 1
    g, fg, acc, sg, keep, send = call(
        functools.partial(feed_first_kernel, steps=first), "feed_first", 5 * first,
        (cot_own, cot_got, kept, second, w_in, w_down),
        [whole()] * 4 + [far()] * 2,
        (wide_bf, wide_bf, wide_f32, wide_f32, *piece_halves(2 * first)),
        grid=first,
        scratch=[vm((first, width, width), BF)] * 2 + [dma((first, 2))],
        vmem=VMEM[1],
        who=who[0],
    )
    a = Piece(calls, keep, send, None, orders[0], rests[0], dp)
    _, _, out_own, out_send, mg, grad_att, gf, *ready = call(
        functools.partial(feed_third_kernel, first), "feed_third", 8,
        (g, fg, acc, sg, kept, middle, second, att, fgain, w_out, w_in, w_down),
        [whole()] * 9 + [far()] * 3,
        (
            wide_f32, wide_f32, row_half, row_half, wide_f32, paired, sds((1, width), F32),
            square_bf, square_bf, square_bf,
        ),
        scratch=[vm((length, width), F32), block, block, block, dma((3,))],
        vmem=VMEM[3],
        aliases={2: 0, 3: 1},
        who=who[0],
    )

    some = sds((rows, pairs // PARTS, length, TILE), BF)
    dq, dk, dv, diag = [], [], [], []
    a.land()
    for part in range(PARTS):
        base = part * (pairs // PARTS)
        outs = call(
            functools.partial(backward_kernel, base=base), "attend_backward", 12 / PARTS,
            (e, q, k, v, inv, att, grad_att),
            [pl.BlockSpec((rows, 1, 2, length, length), lambda p, base=base: (0, p + base, 0, 0, 0))] + [whole()] * 6,
            (some, some, some, sds((heads // PARTS, 1, 2 * length), F32)),
            grid=pairs // PARTS,
            scratch=[vm((2, TILE, 2 * length), F32)],
            vmem=VMEM[4],
        )
        for kept_list, out in zip((dq, dk, dv, diag), outs):
            kept_list.append(out)
        if part == 1:
            a.land()
    keep, send, small = call(
        functools.partial(weight_kernel, PARTS, bucket_count), "weight_grads", 3,
        (normed, *dq, *dk, *dv, *diag, gf, *ready, w_query, w_key, w_value, gain),
        [whole()] * (5 + 4 * PARTS) + [far()] * 3 + [whole()],
        (*piece_halves(6, SMALL), sds((SMALL, width), BF)),
        scratch=[block, block, block, dma((3,))],
        vmem=VMEM[5],
        who=who[1],
    )
    c_piece = Piece(calls, keep, send, small, orders[1], rests[1], dp)
    a.land()
    in_own, in_send = call(
        functools.partial(input_kernel, PARTS), "input_grad", 4,
        (x, mg, *dq, *dk, *dv, w_query, w_key, w_value, gain),
        [whole()] * (2 + 3 * PARTS) + [far()] * 3 + [whole()],
        (row_half, row_half),
        scratch=[vm((length, width), F32), block, block, block, dma((3,))],
        vmem=VMEM[6],
        who=who[0],
    )
    out_got = swap(out_send)
    in_got = swap(in_send)
    grad_down = None
    all_rows = sds((rows, slots, half, width), BF)
    while len(c_piece.steps) > 1:
        c_piece.land()
        if len(a.steps) > 1:
            a.land()
        elif grad_down is None:
            grad_down, grad_in = call(
                feed_result_kernel, "feed_result", 4, a.done(), [whole()] * 2,
                (sds((ff, width), F32), sds((width, ff), F32)),
                out_specs=[far(), far()],
                scratch=[vm((2 * first, width, width), F32), dma((2 * first,))],
                vmem=VMEM[7],
                who=who[0],
            )
            output, grad_input = call(
                place_kernel, "place", 1, (out_own, out_got, in_own, in_got), [whole()] * 4,
                (all_rows, all_rows), out_specs=[far(), far()], scratch=[dma((4 * rows,))], who=who[0],
            )
    grad_down, grad_in, grad_out, grad_query, grad_key, grad_value, ga, gf, grad_table = call(
        rest_result_kernel, "rest_result", 3,
        (*c_piece.done(), grad_down, grad_in), [whole()] * 2 + [far()] * 2,
        (
            sds((ff, width), F32), sds((width, ff), F32), square, square, square, square,
            sds((1, width), F32), sds((1, width), F32), sds((bucket_count, heads), F32),
        ),
        out_specs=[far()] * 6 + [whole()] * 3,
        scratch=[vm((6, width, width), F32), dma((6,))],
        vmem=VMEM[7],
        aliases={2: 0, 3: 1},
        who=who[1],
    )

    return (
        output,
        grad_input,
        ga.reshape(width),
        grad_query,
        grad_key,
        grad_value,
        grad_out,
        gf.reshape(width),
        grad_in,
        grad_down,
        grad_table,
    )


def solution(mesh):
    placed = (P(None, "dp", "seq", None),) * 2 + (P(None, "dp", "seq"),) * 2 + (P(None, "dp"),) + (P(),) * 9
    return jax.shard_map(
        on_device,
        mesh=mesh,
        in_specs=placed,
        out_specs=(P(None, "dp", "seq", None),) * 2 + (P(),) * 9,
        check_vma=False,
    )
```

profile of v0, /device:TPU:0, one launch (start us, length us, event | category | flops | bytes accessed | tf_op | source)
XLA Modules:
  0.0 168.1 jit_solution(9081629873886083109)
XLA Ops:
  2.0 1.6 pick.1
  4.3 2.0 %pick_rest.1 = (bf16[2,256,512]{2,1,0:T(8,128)(2,1)S(1)}, bf16[2,256,512]{2,1,0:T(8,128)(2,1)S(1)}, bf16[2,256,512]{2,1,0:T(8,128)(2,1)S(1)}, f32[8,128]{1,0:T(8,128)}) custom-call(bf16[2,2,256,512]{3,2,1,0:T(8,128)(2,1)} %refs_0_.3, bf16[2,2,256,512]{3,2,1,0:T(8,128)(2,1)} %refs_1_.2), custom_call_target="tpu_custom_call" | custom-call | flops 1000000000 | bytes 1000000 | tf_op jit(solution)/shard_map/pick_rest/pallas_call | solution.py:58
  7.0 16.4 %attend_forward.1 = (bf16[2,512,512]{2,1,0:T(8,128)(2,1)S(1)}, bf16[2,512,512]{2,1,0:T(8,128)(2,1)S(1)}, bf16[2,4,512,128]{3,2,1,0:T(8,128)(2,1)S(1)}, bf16[2,4,...) custom-call(s32[2]{0:T(128)S(1)} %bitcast.11, ...), custom_call_target="tpu_custom_call" | custom-call | flops 14000000000 | bytes 14000000 | tf_op jit(solution)/shard_map/attend_forward/pallas_call | solution.py:58
  23.5 16.8 %feed_first.1 = (bf16[2,512,512]{2,1,0:T(8,128)(2,1)S(1)}, bf16[2,512,512]{2,1,0:T(8,128)(2,1)S(1)}, f32[2,512,512]{2,1,0:T(8,128)S(1)}, f32[2,512,512]{2,1,0:T(...) custom-call(bf16[2,256,512]{2,1,0:T(8,128)(2,1)S(1)} %get-tuple-element.119.refs_0_, ...), custom_call_target="tpu_custom_call" | custom-call | flops 15000000512 | bytes 15000000 | tf_op jit(solution)/shard_map/feed_first/pallas_call | solution.py:58
  40.4 8.5 %feed_third.1 = (f32[2,512,512]{2,1,0:T(8,128)S(1)}, f32[2,512,512]{2,1,0:T(8,128)S(1)}, bf16[2,256,512]{2,1,0:T(8,128)(2,1)S(1)}, bf16[2,256,512]{2,1,0:T(8,128...) custom-call(bf16[2,512,512]{2,1,0:T(8,128)(2,1)S(1)} %get-tuple-elem, ...), custom_call_target="tpu_custom_call", output_to_operand_aliasing={{0}: (2, {}), {1}: (3, {})} | custom-call | flops 8000000000 | bytes 8000000 | tf_op jit(solution)/shard_map/feed_third/pallas_call | solution.py:58
  49.3 3.0 %collective-permute-start.5 = (bf16[768,512]{1,0:T(8,128)(2,1)S(1)}, bf16[768,512]{1,0:T(8,128)(2,1)S(1)}, u32[]{:S(2)}, u32[]{:S(2)}) collective-permute-start(bf16[768,512]{1,0:T(8,128)(2,1)S(1)} %get-tuple-element.155), channel_id=1, source_target_pairs={{0,2},{1,9},{2,0},{3,11},{4,6},{5,13},{6,4},{7,15},{8,10},{9,1},{1... | collective-permute-start | bytes 2359304 | tf_op jit(solution)/shard_map/ppermute | solution.py:589
  52.3 6.0 %attend_backward.2 = (bf16[2,2,512,128]{3,2,1,0:T(8,128)(2,1)S(1)}, bf16[2,2,512,128]{3,2,1,0:T(8,128)(2,1)S(1)}, bf16[2,2,512,128]{3,2,1,0:T(8,128)(2,1)S(1)}, f32[4,1,1024]{2,1,0:T(1,128)S(1)}, f32[8,128]{1,0:T(8,128)S(1)}) custom-call(bf16[2,4,2,512,512]{4,3,2,1,0:T(8,128)(2,1)S(1)} %get-tuple-element.137.refs_0_, ...), custom_call_target="tpu_custom_call" | custom-call | flops 6000000000 | bytes 6000000 | tf_op jit(solution)/shard_map/attend_backward/pallas_call | solution.py:58
  58.3 6.3 %attend_backward.3 = (bf16[2,2,512,128]{3,2,1,0:T(8,128)(2,1)S(1)}, bf16[2,2,512,128]{3,2,1,0:T(8,128)(2,1)S(1)}, bf16[2,2,512,128]{3,2,1,0:T(8,128)(2,1)S(1)}, f32[4,1,1024]{2,1,0:T(1,128)S(1)}, f32[8,128]{1,0:T(8,128)S(1)}) custom-call(bf16[2,4,2,512,512]{4,3,2,1,0:T(8,128)(2,1)S(1)} %get-tuple-element.137.refs_0_, ...), custom_call_target="tpu_custom_call" | custom-call | flops 6000000000 | bytes 6000000 | tf_op jit(solution)/shard_map/attend_backward/pallas_call | solution.py:58
  64.8 4.1 %weight_grads.1 = (bf16[1536,512]{1,0:T(8,128)(2,1)S(1)}, bf16[1568,512]{1,0:T(8,128)(2,1)S(1)}, bf16[32,512]{1,0:T(8,128)(2,1)S(1)}, f32[8,128]{1,0:T(8,128)S(1)}) custom-call(bf16[2,512,512]{2,1,0:T(8,128)(2,1)S(1)} %get-tuple-element.159.refs_0_, bf16[2,2,512,128]{3,2,1,0:T(8,128)(2,1)S(1)} %get-tuple-element.147.refs_1_.refs_2_, ...), custom_call_target="tpu_custom_call" | custom-call | flops 3000000000 | bytes 3000000 | tf_op jit(solution)/shard_map/weight_grads/pallas_call | solution.py:58
  68.9 1.6 collective-permute-start.6
  70.5 6.3 %collective-permute-done.6.refs_1_ = bf16[384,512]{1,0:T(8,128)(2,1)S(1)} collective-permute-done((bf16[384,512]{1,0:T(8,128)(2,1)S(1)}, bf16[384,512]{1,0:T(8,128)(2,1)S(1)}, u32[]{:S(2)}, u32[]{:S(2)}) %collective-permute-start.6) | collective-permute-done | bytes 393248 | tf_op jit(solution)/shard_map/ppermute | solution.py:589
  76.9 3.7 %input_grad.1 = (bf16[2,256,512]{2,1,0:T(8,128)(2,1)S(1)}, bf16[2,256,512]{2,1,0:T(8,128)(2,1)S(1)}, f32[8,128]{1,0:T(8,128)S(1)}) custom-call(bf16[2,512,512]{2,1,0:T(8,128)(2,1)S(1)} %get-tuple-element.135.refs_0_, f32[2,512,512]{2,1,0:T(8,128)S(1)} %get-tuple-element.136.refs_1_, bf16[2,2,512,128]{3,2,1,0:T(8,128)(2,1)S(1)} %get-tuple-element.147.refs_1_.refs_2_, ...), custom_call_target="tpu_custom_call" | custom-call | flops 4000000000 | bytes 4000000 | tf_op jit(solution)/shard_map/input_grad/pallas_call | solution.py:58
  81.0 1.6 collective-permute-start.11
  82.6 1.6 collective-permute-start.8
  84.2 4.1 %collective-permute-done.8.refs_1_ = bf16[192,512]{1,0:T(8,128)(2,1)S(1)} collective-permute-done((bf16[192,512]{1,0:T(8,128)(2,1)S(1)}, bf16[192,512]{1,0:T(8,128)(2,1)S(1)}, u32[]{:S(2)}, u32[]{:S(2)}) %collective-permute-start.8) | collective-permute-done | bytes 196640 | tf_op jit(solution)/shard_map/ppermute | solution.py:589
  88.3 6.5 %collective-permute-done.11.refs_1_ = bf16[800,512]{1,0:T(8,128)(2,1)S(1)} collective-permute-done((bf16[800,512]{1,0:T(8,128)(2,1)S(1)}, bf16[800,512]{1,0:T(8,128)(2,1)S(1)}, u32[]{:S(2)}, u32[]{:S(2)}) %collective-permute-start.11) | collective-permute-done | bytes 819232 | tf_op jit(solution)/shard_map/ppermute | solution.py:589
  96.2 2.6 %collective-permute-start.10 = (bf16[192,512]{1,0:T(8,128)(2,1)S(1)}, bf16[192,512]{1,0:T(8,128)(2,1)S(1)}, u32[]{:S(2)}, u32[]{:S(2)}) collective-permute-start(bf16[192,512]{1,0:T(8,128)(2,1)S(1)} %get-tuple-element.178.refs_0_), channel_id=1, source_target_pairs={{0,16},{1,17},{2,18},{3,19},{4,20},{5,21},{6,22},{7,23},{8,24},{9,... | collective-permute-start | bytes 589832 | tf_op jit(solution)/shard_map/ppermute | solution.py:589
  98.8 6.3 %collective-permute-done.10.refs_1_ = bf16[192,512]{1,0:T(8,128)(2,1)S(1)} collective-permute-done((bf16[192,512]{1,0:T(8,128)(2,1)S(1)}, bf16[192,512]{1,0:T(8,128)(2,1)S(1)}, u32[]{:S(2)}, u32[]{:S(2)}) %collective-permute-start.10) | collective-permute-done | bytes 196640 | tf_op jit(solution)/shard_map/ppermute | solution.py:589
  105.2 2.9 %collective-permute-start.12 = (bf16[192,512]{1,0:T(8,128)(2,1)S(1)}, bf16[192,512]{1,0:T(8,128)(2,1)S(1)}, u32[]{:S(2)}, u32[]{:S(2)}) collective-permute-start(bf16[192,512]{1,0:T(8,128)(2,1)S(1)} %get-tuple-element.184.refs_0_), channel_id=1, source_target_pairs={{0,8},{1,5},{2,10},{3,7},{4,12},{5,1},{6,14},{7,3},{8,0},{9,13},{1... | collective-permute-start | bytes 589832 | tf_op jit(solution)/shard_map/ppermute | solution.py:589
  108.1 5.6 %collective-permute-done.12.refs_1_ = bf16[192,512]{1,0:T(8,128)(2,1)S(1)} collective-permute-done((bf16[192,512]{1,0:T(8,128)(2,1)S(1)}, bf16[192,512]{1,0:T(8,128)(2,1)S(1)}, u32[]{:S(2)}, u32[]{:S(2)}) %collective-permute-start.12) | collective-permute-done | bytes 196640 | tf_op jit(solution)/shard_map/ppermute | solution.py:589
  114.8 1.6 collective-permute-start.15
  116.3 4.4 %collective-permute-done.15.refs_1_ = bf16[224,512]{1,0:T(8,128)(2,1)S(1)} collective-permute-done((bf16[224,512]{1,0:T(8,128)(2,1)S(1)}, bf16[224,512]{1,0:T(8,128)(2,1)S(1)}, u32[]{:S(2)}, u32[]{:S(2)}) %collective-permute-start.15) | collective-permute-done | bytes 229408 | tf_op jit(solution)/shard_map/ppermute | solution.py:589
  122.6 2.2 %collective-permute-start.17 = (bf16[224,512]{1,0:T(8,128)(2,1)S(1)}, bf16[224,512]{1,0:T(8,128)(2,1)S(1)}, u32[]{:S(2)}, u32[]{:S(2)}) collective-permute-start(bf16[224,512]{1,0:T(8,128)(2,1)S(1)} %get-tuple-element.198), channel_id=1, source_target_pairs={{0,16},{1,17},{2,18},{3,19},{4,20},{5,21},{6,22},{7,23},{8,24},{9,... | collective-permute-start | bytes 688136 | tf_op jit(solution)/shard_map/ppermute | solution.py:589
  124.7 9.7 %collective-permute-done.17.refs_1_ = bf16[224,512]{1,0:T(8,128)(2,1)S(1)} collective-permute-done((bf16[224,512]{1,0:T(8,128)(2,1)S(1)}, bf16[224,512]{1,0:T(8,128)(2,1)S(1)}, u32[]{:S(2)}, u32[]{:S(2)}) %collective-permute-start.17) | collective-permute-done | bytes 229408 | tf_op jit(solution)/shard_map/ppermute | solution.py:589
  134.7 1.3 collective-permute-start.19
  136.4 4.0 %collective-permute-done.19.refs_1_ = bf16[192,512]{1,0:T(8,128)(2,1)S(1)} collective-permute-done((bf16[192,512]{1,0:T(8,128)(2,1)S(1)}, bf16[192,512]{1,0:T(8,128)(2,1)S(1)}, u32[]{:S(2)}, u32[]{:S(2)}) %collective-permute-start.19) | collective-permute-done | bytes 196640 | tf_op jit(solution)/shard_map/ppermute | solution.py:589
  141.5 2.8 %feed_result.1 = (f32[2048,512]{1,0:T(8,128)}, f32[512,2048]{1,0:T(8,128)}, f32[8,128]{1,0:T(8,128)S(1)}) custom-call(bf16[1536,512]{1,0:T(8,128)(2,1)S(1)} %get-tuple-element.202.refs_0_, bf16[1536,512]{1,0:T(8,128)(2,1)S(1)} %collective-permute-done.18.refs_1_, f32[8,128]{1,0:T(8,128)S(1)} %get-tuple-element.205.refs_2_), custom_call_target="tpu_custom_call" | custom-call | flops 4000000000 | bytes 4000000 | tf_op jit(solution)/shard_map/feed_result/pallas_call | solution.py:58
  144.3 1.4 place.1
  145.7 2.6 %collective-permute-done.20.refs_1_ = bf16[384,512]{1,0:T(8,128)(2,1)S(1)} collective-permute-done((bf16[384,512]{1,0:T(8,128)(2,1)S(1)}, bf16[384,512]{1,0:T(8,128)(2,1)S(1)}, u32[]{:S(2)}, u32[]{:S(2)}) %collective-permute-start.20) | collective-permute-done | bytes 393248 | tf_op jit(solution)/shard_map/ppermute | solution.py:589
  149.1 11.2 %collective-permute-done.21.refs_1_ = bf16[768,512]{1,0:T(8,128)(2,1)S(1)} collective-permute-done((bf16[768,512]{1,0:T(8,128)(2,1)S(1)}, bf16[768,512]{1,0:T(8,128)(2,1)S(1)}, u32[]{:S(2)}, u32[]{:S(2)}) %collective-permute-start.21) | collective-permute-done | bytes 786464 | tf_op jit(solution)/shard_map/ppermute | solution.py:589
  160.6 3.4 %collective-permute-done.22.refs_1_ = bf16[1568,512]{1,0:T(8,128)(2,1)S(1)} collective-permute-done((bf16[1568,512]{1,0:T(8,128)(2,1)S(1)}, bf16[1568,512]{1,0:T(8,128)(2,1)S(1)}, u32[]{:S(2)}, u32[]{:S(2)}) %collective-permute-start.22) | collective-permute-done | bytes 1605664 | tf_op jit(solution)/shard_map/ppermute | solution.py:589
  164.0 3.4 %rest_result.1 = (f32[2048,512]{1,0:T(8,128)}, f32[512,2048]{1,0:T(8,128)}, f32[512,512]{1,0:T(8,128)}, f32[512,512]{1,0:T(8,128)}, f32[512,512]{1,0:T(8,128)}, ...) custom-call(bf16[1568,512]{1,0:T(8,128)(2,1)S(1)} %get-tuple-element, ...), custom_call_target="tpu_custom_call", output_to_operand_aliasing={{0}: (2, {}), {1}: (3, {})} | custom-call | flops 3000000000 | bytes 3000000 | tf_op jit(solution)/shard_map/rest_result/pallas_call | solution.py:58
  (56 shorter events, 11.8 us)
Async XLA Ops:
  0.6 0.7 copy-start
  1.3 0.7 copy-start.1
  3.7 3.1 %copy-start.5 = (f32[32,8]{0,1:T(8,128)S(1)}, f32[32,8]{0,1:T(8,128)}, u32[]{:S(2)}) copy-start(f32[32,8]{0,1:T(8,128)} %param.27) | copy-start | bytes 3076
  3.7 3.3 %copy-start.2 = (f32[512]{0:T(512)S(1)}, f32[512]{0:T(512)}, u32[]{:S(2)}) copy-start(f32[512]{0:T(512)} %param.24) | copy-start | bytes 6148
  3.7 3.3 %copy-start.3 = (f32[512]{0:T(512)S(1)}, f32[512]{0:T(512)}, u32[]{:S(2)}) copy-start(f32[512]{0:T(512)} %param.19) | copy-start | bytes 6148
  3.7 3.3 %copy-start.4 = (s32[2,1]{0,1:T(1,128)S(1)}, s32[2,1]{0,1:T(1,128)}, u32[]{:S(2)}) copy-start(s32[2,1]{0,1:T(1,128)} %param.18) | copy-start | bytes 28
  3.7 3.2 %collective-permute-start.1 = (bf16[2,256,512]{2,1,0:T(8,128)(2,1)S(1)}, bf16[2,256,512]{2,1,0:T(8,128)(2,1)S(1)}, u32[]{:S(2)}, u32[]{:S(2)}) collective-permute-start(bf16[2,256,512]{2,1,0:T(8,128)(2,1)S(1)} %get-tuple-element.122), channel_id=1, source_target_pairs={{0,1},{1,0},{2,3},{3,2},{4,5},{5,4},{6,7},{7,6},{8,9},{9,8},{10,11... | collective-permute-start | bytes 1572872 | tf_op jit(solution)/shard_map/ppermute | solution.py:658
  4.2 2.7 %collective-permute-start.2 = (s32[2,2,256]{2,1,0:T(2,128)S(1)}, s32[2,2,256]{2,1,0:T(2,128)S(1)}, u32[]{:S(2)}, u32[]{:S(2)}) collective-permute-start(s32[2,2,256]{2,1,0:T(2,128)S(1)} %get-tuple-element.124), channel_id=1, source_target_pairs={{0,1},{1,0},{2,3},{3,2},{4,5},{5,4},{6,7},{7,6},{8,9},{9,8},{10,11... | collective-permute-start | bytes 12296 | tf_op jit(solution)/shard_map/ppermute | solution.py:658
  6.3 17.1 %collective-permute-start = (bf16[2,256,512]{2,1,0:T(8,128)(2,1)S(1)}, bf16[2,256,512]{2,1,0:T(8,128)(2,1)S(1)}, u32[]{:S(2)}, u32[]{:S(2)}) collective-permute-start(bf16[2,256,512]{2,1,0:T(8,128)(2,1)S(1)} %get-tuple-element.120), channel_id=1, source_target_pairs={{0,1},{1,0},{2,3},{3,2},{4,5},{5,4},{6,7},{7,6},{8,9},{9,8},{10,11... | collective-permute-start | bytes 1572872 | tf_op jit(solution)/shard_map/ppermute | solution.py:658
  40.3 8.6 %collective-permute-start.4 = (bf16[1536,512]{1,0:T(8,128)(2,1)S(1)}, bf16[1536,512]{1,0:T(8,128)(2,1)S(1)}, u32[]{:S(2)}, u32[]{:S(2)}) collective-permute-start(bf16[1536,512]{1,0:T(8,128)(2,1)S(1)} %get-tuple-element.144), channel_id=1, source_target_pairs={{0,1},{1,0},{2,3},{3,2},{4,5},{5,4},{6,7},{7,6},{8,9},{9,8},{10,11... | collective-permute-start | bytes 4718600 | tf_op jit(solution)/shard_map/ppermute | solution.py:589
  49.3 15.3 %collective-permute-start.5 = (bf16[768,512]{1,0:T(8,128)(2,1)S(1)}, bf16[768,512]{1,0:T(8,128)(2,1)S(1)}, u32[]{:S(2)}, u32[]{:S(2)}) collective-permute-start(bf16[768,512]{1,0:T(8,128)(2,1)S(1)} %get-tuple-element.155), channel_id=1, source_target_pairs={{0,2},{1,9},{2,0},{3,11},{4,6},{5,13},{6,4},{7,15},{8,10},{9,1},{1... | collective-permute-start | bytes 2359304 | tf_op jit(solution)/shard_map/ppermute | solution.py:589
  68.8 11.8 %collective-permute-start.9 = (bf16[1568,512]{1,0:T(8,128)(2,1)S(1)}, bf16[1568,512]{1,0:T(8,128)(2,1)S(1)}, u32[]{:S(2)}, u32[]{:S(2)}) collective-permute-start(bf16[1568,512]{1,0:T(8,128)(2,1)S(1)} %get-tuple-element.174), channel_id=1, source_target_pairs={{0,1},{1,0},{2,3},{3,2},{4,5},{5,4},{6,7},{7,6},{8,9},{9,8},{10,11... | collective-permute-start | bytes 4816904 | tf_op jit(solution)/shard_map/ppermute | solution.py:589
  68.9 7.8 %collective-permute-start.6 = (bf16[384,512]{1,0:T(8,128)(2,1)S(1)}, bf16[384,512]{1,0:T(8,128)(2,1)S(1)}, u32[]{:S(2)}, u32[]{:S(2)}) collective-permute-start(bf16[384,512]{1,0:T(8,128)(2,1)S(1)} %get-tuple-element.158), channel_id=1, source_target_pairs={{0,4},{1,3},{2,6},{3,1},{4,0},{5,7},{6,2},{7,5},{8,12},{9,11},{10,... | collective-permute-start | bytes 1179656 | tf_op jit(solution)/shard_map/ppermute | solution.py:589
  81.0 13.8 %collective-permute-start.11 = (bf16[800,512]{1,0:T(8,128)(2,1)S(1)}, bf16[800,512]{1,0:T(8,128)(2,1)S(1)}, u32[]{:S(2)}, u32[]{:S(2)}) collective-permute-start(bf16[800,512]{1,0:T(8,128)(2,1)S(1)} %get-tuple-element.180), channel_id=1, source_target_pairs={{0,4},{1,3},{2,6},{3,1},{4,0},{5,7},{6,2},{7,5},{8,12},{9,11},{10,... | collective-permute-start | bytes 2457608 | tf_op jit(solution)/shard_map/ppermute | solution.py:589
  82.6 5.7 %collective-permute-start.8 = (bf16[192,512]{1,0:T(8,128)(2,1)S(1)}, bf16[192,512]{1,0:T(8,128)(2,1)S(1)}, u32[]{:S(2)}, u32[]{:S(2)}) collective-permute-start(bf16[192,512]{1,0:T(8,128)(2,1)S(1)} %get-tuple-element.172), channel_id=1, source_target_pairs={{0,8},{1,5},{2,10},{3,7},{4,12},{5,1},{6,14},{7,3},{8,0},{9,13},{1... | collective-permute-start | bytes 589832 | tf_op jit(solution)/shard_map/ppermute | solution.py:589
  95.0 13.0 %collective-permute-start.13 = (bf16[416,512]{1,0:T(8,128)(2,1)S(1)}, bf16[416,512]{1,0:T(8,128)(2,1)S(1)}, u32[]{:S(2)}, u32[]{:S(2)}) collective-permute-start(bf16[416,512]{1,0:T(8,128)(2,1)S(1)} %get-tuple-element.186), channel_id=1, source_target_pairs={{0,8},{1,5},{2,10},{3,7},{4,12},{5,1},{6,14},{7,3},{8,0},{9,13},{1... | collective-permute-start | bytes 1277960 | tf_op jit(solution)/shard_map/ppermute | solution.py:589
  96.2 8.9 %collective-permute-start.10 = (bf16[192,512]{1,0:T(8,128)(2,1)S(1)}, bf16[192,512]{1,0:T(8,128)(2,1)S(1)}, u32[]{:S(2)}, u32[]{:S(2)}) collective-permute-start(bf16[192,512]{1,0:T(8,128)(2,1)S(1)} %get-tuple-element.178.refs_0_), channel_id=1, source_target_pairs={{0,16},{1,17},{2,18},{3,19},{4,20},{5,21},{6,22},{7,23},{8,24},{9,... | collective-permute-start | bytes 589832 | tf_op jit(solution)/shard_map/ppermute | solution.py:589
  105.2 8.6 %collective-permute-start.12 = (bf16[192,512]{1,0:T(8,128)(2,1)S(1)}, bf16[192,512]{1,0:T(8,128)(2,1)S(1)}, u32[]{:S(2)}, u32[]{:S(2)}) collective-permute-start(bf16[192,512]{1,0:T(8,128)(2,1)S(1)} %get-tuple-element.184.refs_0_), channel_id=1, source_target_pairs={{0,8},{1,5},{2,10},{3,7},{4,12},{5,1},{6,14},{7,3},{8,0},{9,13},{1... | collective-permute-start | bytes 589832 | tf_op jit(solution)/shard_map/ppermute | solution.py:589
  113.8 7.8 %collective-permute-start.14 = (bf16[384,512]{1,0:T(8,128)(2,1)S(1)}, bf16[384,512]{1,0:T(8,128)(2,1)S(1)}, u32[]{:S(2)}, u32[]{:S(2)}) collective-permute-start(bf16[384,512]{1,0:T(8,128)(2,1)S(1)} %get-tuple-element.190.refs_0_), channel_id=1, source_target_pairs={{0,4},{1,3},{2,6},{3,1},{4,0},{5,7},{6,2},{7,5},{8,12},{9,11},{10,... | collective-permute-start | bytes 1179656 | tf_op jit(solution)/shard_map/ppermute | solution.py:589
  114.8 6.0 %collective-permute-start.15 = (bf16[224,512]{1,0:T(8,128)(2,1)S(1)}, bf16[224,512]{1,0:T(8,128)(2,1)S(1)}, u32[]{:S(2)}, u32[]{:S(2)}) collective-permute-start(bf16[224,512]{1,0:T(8,128)(2,1)S(1)} %get-tuple-element.192), channel_id=1, source_target_pairs={{0,2},{1,9},{2,0},{3,11},{4,6},{5,13},{6,4},{7,15},{8,10},{9,1},{1... | collective-permute-start | bytes 688136 | tf_op jit(solution)/shard_map/ppermute | solution.py:589
  121.7 12.8 %collective-permute-start.16 = (bf16[768,512]{1,0:T(8,128)(2,1)S(1)}, bf16[768,512]{1,0:T(8,128)(2,1)S(1)}, u32[]{:S(2)}, u32[]{:S(2)}) collective-permute-start(bf16[768,512]{1,0:T(8,128)(2,1)S(1)} %get-tuple-element.196.refs_0_), channel_id=1, source_target_pairs={{0,2},{1,9},{2,0},{3,11},{4,6},{5,13},{6,4},{7,15},{8,10},{9,1},{1... | collective-permute-start | bytes 2359304 | tf_op jit(solution)/shard_map/ppermute | solution.py:589
  122.6 11.8 %collective-permute-start.17 = (bf16[224,512]{1,0:T(8,128)(2,1)S(1)}, bf16[224,512]{1,0:T(8,128)(2,1)S(1)}, u32[]{:S(2)}, u32[]{:S(2)}) collective-permute-start(bf16[224,512]{1,0:T(8,128)(2,1)S(1)} %get-tuple-element.198), channel_id=1, source_target_pairs={{0,16},{1,17},{2,18},{3,19},{4,20},{5,21},{6,22},{7,23},{8,24},{9,... | collective-permute-start | bytes 688136 | tf_op jit(solution)/shard_map/ppermute | solution.py:589
  134.6 6.9 %collective-permute-start.18 = (bf16[1536,512]{1,0:T(8,128)(2,1)S(1)}, bf16[1536,512]{1,0:T(8,128)(2,1)S(1)}, u32[]{:S(2)}, u32[]{:S(2)}) collective-permute-start(bf16[1536,512]{1,0:T(8,128)(2,1)S(1)} %get-tuple-element.202.refs_0_), channel_id=1, source_target_pairs={{0,1},{1,0},{2,3},{3,2},{4,5},{5,4},{6,7},{7,6},{8,9},{9,8},{10,11... | collective-permute-start | bytes 4718600 | tf_op jit(solution)/shard_map/ppermute | solution.py:589
  134.7 5.7 %collective-permute-start.19 = (bf16[192,512]{1,0:T(8,128)(2,1)S(1)}, bf16[192,512]{1,0:T(8,128)(2,1)S(1)}, u32[]{:S(2)}, u32[]{:S(2)}) collective-permute-start(bf16[192,512]{1,0:T(8,128)(2,1)S(1)} %get-tuple-element.203.refs_0_), channel_id=1, source_target_pairs={{0,2},{1,9},{2,0},{3,11},{4,6},{5,13},{6,4},{7,15},{8,10},{9,1},{1... | collective-permute-start | bytes 589832 | tf_op jit(solution)/shard_map/ppermute | solution.py:589
  135.9 8.4 %collective-permute-start.3 = (bf16[2,256,512]{2,1,0:T(8,128)(2,1)S(1)}, bf16[2,256,512]{2,1,0:T(8,128)(2,1)S(1)}, u32[]{:S(2)}, u32[]{:S(2)}) collective-permute-start(bf16[2,256,512]{2,1,0:T(8,128)(2,1)S(1)} %get-tuple-element.134), channel_id=1, source_target_pairs={{0,1},{1,0},{2,3},{3,2},{4,5},{5,4},{6,7},{7,6},{8,9},{9,8},{10,11... | collective-permute-start | bytes 1572872 | tf_op jit(solution)/shard_map/ppermute | solution.py:658
  135.9 8.4 %collective-permute-start.7 = (bf16[2,256,512]{2,1,0:T(8,128)(2,1)S(1)}, bf16[2,256,512]{2,1,0:T(8,128)(2,1)S(1)}, u32[]{:S(2)}, u32[]{:S(2)}) collective-permute-start(bf16[2,256,512]{2,1,0:T(8,128)(2,1)S(1)} %get-tuple-element.170), channel_id=1, source_target_pairs={{0,1},{1,0},{2,3},{3,2},{4,5},{5,4},{6,7},{7,6},{8,9},{9,8},{10,11... | collective-permute-start | bytes 1572872 | tf_op jit(solution)/shard_map/ppermute | solution.py:658
  140.4 7.8 %collective-permute-start.20 = (bf16[384,512]{1,0:T(8,128)(2,1)S(1)}, bf16[384,512]{1,0:T(8,128)(2,1)S(1)}, u32[]{:S(2)}, u32[]{:S(2)}) collective-permute-start(bf16[384,512]{1,0:T(8,128)(2,1)S(1)} %get-tuple-element.209.refs_0_), channel_id=1, source_target_pairs={{0,8},{1,5},{2,10},{3,7},{4,12},{5,1},{6,14},{7,3},{8,0},{9,13},{1... | collective-permute-start | bytes 1179656 | tf_op jit(solution)/shard_map/ppermute | solution.py:589
  148.3 12.1 %collective-permute-start.21 = (bf16[768,512]{1,0:T(8,128)(2,1)S(1)}, bf16[768,512]{1,0:T(8,128)(2,1)S(1)}, u32[]{:S(2)}, u32[]{:S(2)}) collective-permute-start(bf16[768,512]{1,0:T(8,128)(2,1)S(1)} %get-tuple-element.211.refs_0_), channel_id=1, source_target_pairs={{0,4},{1,3},{2,6},{3,1},{4,0},{5,7},{6,2},{7,5},{8,12},{9,11},{10,... | collective-permute-start | bytes 2359304 | tf_op jit(solution)/shard_map/ppermute | solution.py:589
  160.5 3.5 %collective-permute-start.22 = (bf16[1568,512]{1,0:T(8,128)(2,1)S(1)}, bf16[1568,512]{1,0:T(8,128)(2,1)S(1)}, u32[]{:S(2)}, u32[]{:S(2)}) collective-permute-start(bf16[1568,512]{1,0:T(8,128)(2,1)S(1)} %get-tuple-element.214.refs_0_), channel_id=1, source_target_pairs={{0,1},{1,0},{2,3},{3,2},{4,5},{5,4},{6,7},{7,6},{8,9},{9,8},{10,11... | collective-permute-start | bytes 4816904 | tf_op jit(solution)/shard_map/ppermute | solution.py:589
where the time goes:
time: 168 us
  Pallas kernels  74.9 us (45%)
  waiting for transfers between devices  64.9 us (39%)
  starting transfers between devices  25.1 us (15%)
  local copies, waits for them, and re-layouts  2.19 us (1%)
    pallas_call x28, Pallas kernels, call(): pl.pallas_call(body, grid=(grid,), in_specs=list(in_specs) + [whole()] *...  74.9 us
    ppermute x18, waiting for transfers between devices, fly(): lax.ppermute(self.send, ('dp', 'seq'), swap_pairs(self.dp, self.steps[0][...  64.9 us
    ppermute x18, starting transfers between devices, fly(): lax.ppermute(self.send, ('dp', 'seq'), swap_pairs(self.dp, self.steps[0][...  23.5 us
  transfers between devices with their start and end apart: 23, of which 12 were waited for; matrix products, arithmetic and copies ran while one was open for 0% of the time, Pallas kernels for 28%

commit v1 on v0

--- a/solution.py
+++ b/solution.py
@@ -17,9 +17,10 @@
 LEVELS = 4
 SPLIT = 2
 SMALL = 32
+COST = 3e9
 PARTS = 2
 FREE = ("pick_rest", "attend_forward", "feed_first", "feed_third")
-ORDERS = ([(0, 2), (1, 0), (2, 1)], [(1, 0), (2, 1), (0, 2)])
+ORDERS = ([(0, 1), (1, 0), (2, 2)], [(1, 0), (0, 1), (2, 2)])
 VMEM = (16, 15, 12, 14, 12, 10, 10, 14)
 
 
@@ -65,7 +66,7 @@
             input_output_aliases=aliases or {},
             compiler_params=pltpu.CompilerParams(vmem_limit_bytes=vmem * 1024 * 1024),
             cost_estimate=pl.CostEstimate(
-                flops=int(micros * 1e9), bytes_accessed=int(micros * 1e6), transcendentals=0
+                flops=int(micros * COST), bytes_accessed=1 << 20, transcendentals=0
             ),
             name=name,
         )(*inputs, *extra)
@@ -746,8 +747,7 @@
         )
         for kept_list, out in zip((dq, dk, dv, diag), outs):
             kept_list.append(out)
-        if part == 1:
-            a.land()
+        a.land()
     keep, send, small = call(
         functools.partial(weight_kernel, PARTS, bucket_count), "weight_grads", 3,
         (normed, *dq, *dk, *dv, *diag, gf, *ready, w_query, w_key, w_value, gain),
@@ -758,7 +758,6 @@
         who=who[1],
     )
     c_piece = Piece(calls, keep, send, small, orders[1], rests[1], dp)
-    a.land()
     in_own, in_send = call(
         functools.partial(input_kernel, PARTS), "input_grad", 4,
         (x, mg, *dq, *dk, *dv, w_query, w_key, w_value, gain),
@@ -768,15 +767,22 @@
         vmem=VMEM[6],
         who=who[0],
     )
+    a.land()
     out_got = swap(out_send)
     in_got = swap(in_send)
     grad_down = None
     all_rows = sds((rows, slots, half, width), BF)
-    while len(c_piece.steps) > 1:
-        c_piece.land()
+    c_piece.land()
+    a.land()
+    c_piece.land()
+    a.land()
+    c_piece.land()
+    while len(a.steps) > 1 or grad_down is None:
+        if len(a.steps) > 1 or len(c_piece.steps) > 1:
+            c_piece.land()
         if len(a.steps) > 1:
             a.land()
-        elif grad_down is None:
+        else:
             grad_down, grad_in = call(
                 feed_result_kernel, "feed_result", 4, a.done(), [whole()] * 2,
                 (sds((ff, width), F32), sds((width, ff), F32)),

time: 168 us -> 159 us (0.946)
  waiting for transfers between devices: 64.9 us -> 55.1 us
    ppermute x18, waiting for transfers between devices: 64.9 us -> 55.1 us  [fly(): lax.ppermute(self.send, ('dp', 'seq'), swap_pairs(self.dp, self.steps[0][...]
  transfers between devices with their start and end apart: 23 -> 23, of which waited for: 12 -> 12; matrix products, arithmetic and copies ran while one was open for 0% -> 0% of each run, Pallas kernels for 28% -> 30%
where the time goes in v1:
time: 159 us
  Pallas kernels  74.4 us (47%)
  waiting for transfers between devices  55.1 us (35%)
  starting transfers between devices  26.1 us (16%)
  local copies, waits for them, and re-layouts  2.18 us (1%)
    pallas_call x28, Pallas kernels, call(): pl.pallas_call(body, grid=(grid,), in_specs=list(in_specs) + [whole()] *...  74.4 us
    ppermute x18, waiting for transfers between devices, fly(): lax.ppermute(self.send, ('dp', 'seq'), swap_pairs(self.dp, self.steps[0][...  55.1 us
    ppermute x18, starting transfers between devices, fly(): lax.ppermute(self.send, ('dp', 'seq'), swap_pairs(self.dp, self.steps[0][...  24.4 us
  transfers between devices with their start and end apart: 23, of which 12 were waited for; matrix products, arithmetic and copies ran while one was open for 0% of the time, Pallas kernels for 30%

profile of v1, /device:TPU:0, one launch (start us, length us, event | category | flops | bytes accessed | tf_op | source)
XLA Modules:
  0.0 158.7 jit_solution(17725929177436098692)
XLA Ops:
  2.0 1.6 %pick.1 = (bf16[2,256,512]{2,1,0:T(8,128)(2,1)S(1)}, s32[2,2,256]{2,1,0:T(2,128)S(1)}, s32[2,2,256]{2,1,0:T(2,128)S(1)}, f32[8,128]{1,0:T(8,128)}) custom-call(bf16[2,2,256,512]{3,2,1,0:T(8,128)(2,1)} %refs_0_.3, s32[2,2,256]{2,1,0:T(2,128)S(1)} %copy-done, s32[2,2,256]{2,1,0:T(2,128)S(1)} %copy-done.1), custom_call_target="tpu_custom_call" | custom-call | flops 3000000000 | bytes 1048576 | tf_op jit(solution)/shard_map/pick/pallas_call | solution.py:59
  4.3 2.0 %pick_rest.1 = (bf16[2,256,512]{2,1,0:T(8,128)(2,1)S(1)}, bf16[2,256,512]{2,1,0:T(8,128)(2,1)S(1)}, bf16[2,256,512]{2,1,0:T(8,128)(2,1)S(1)}, f32[8,128]{1,0:T(8,128)}) custom-call(bf16[2,2,256,512]{3,2,1,0:T(8,128)(2,1)} %refs_0_.3, bf16[2,2,256,512]{3,2,1,0:T(8,128)(2,1)} %refs_1_.2), custom_call_target="tpu_custom_call" | custom-call | flops 3000000000 | bytes 1048576 | tf_op jit(solution)/shard_map/pick_rest/pallas_call | solution.py:59
  7.0 16.4 %attend_forward.1 = (bf16[2,512,512]{2,1,0:T(8,128)(2,1)S(1)}, bf16[2,512,512]{2,1,0:T(8,128)(2,1)S(1)}, bf16[2,4,512,128]{3,2,1,0:T(8,128)(2,1)S(1)}, bf16[2,4,...) custom-call(s32[2]{0:T(128)S(1)} %bitcast.11, ...), custom_call_target="tpu_custom_call" | custom-call | flops 41999998976 | bytes 1048576 | tf_op jit(solution)/shard_map/attend_forward/pallas_call | solution.py:59
  23.5 16.6 %feed_first.1 = (bf16[2,512,512]{2,1,0:T(8,128)(2,1)S(1)}, bf16[2,512,512]{2,1,0:T(8,128)(2,1)S(1)}, f32[2,512,512]{2,1,0:T(8,128)S(1)}, f32[2,512,512]{2,1,0:T(...) custom-call(bf16[2,256,512]{2,1,0:T(8,128)(2,1)S(1)} %get-tuple-element.119.refs_0_, ...), custom_call_target="tpu_custom_call" | custom-call | flops 44999999488 | bytes 1048576 | tf_op jit(solution)/shard_map/feed_first/pallas_call | solution.py:59
  40.2 8.4 %feed_third.1 = (f32[2,512,512]{2,1,0:T(8,128)S(1)}, f32[2,512,512]{2,1,0:T(8,128)S(1)}, bf16[2,256,512]{2,1,0:T(8,128)(2,1)S(1)}, bf16[2,256,512]{2,1,0:T(8,128...) custom-call(bf16[2,512,512]{2,1,0:T(8,128)(2,1)S(1)} %get-tuple-elem, ...), custom_call_target="tpu_custom_call", output_to_operand_aliasing={{0}: (2, {}), {1}: (3, {})} | custom-call | flops 24000000000 | bytes 1048576 | tf_op jit(solution)/shard_map/feed_third/pallas_call | solution.py:59
  48.9 3.0 %collective-permute-start.5 = (bf16[768,512]{1,0:T(8,128)(2,1)S(1)}, bf16[768,512]{1,0:T(8,128)(2,1)S(1)}, u32[]{:S(2)}, u32[]{:S(2)}) collective-permute-start(bf16[768,512]{1,0:T(8,128)(2,1)S(1)} %get-tuple-element.149), channel_id=1, source_target_pairs={{0,2},{1,5},{2,0},{3,7},{4,6},{5,1},{6,4},{7,3},{8,10},{9,13},{10,... | collective-permute-start | bytes 2359304 | tf_op jit(solution)/shard_map/ppermute | solution.py:590
  51.9 6.0 %attend_backward.2 = (bf16[2,2,512,128]{3,2,1,0:T(8,128)(2,1)S(1)}, bf16[2,2,512,128]{3,2,1,0:T(8,128)(2,1)S(1)}, bf16[2,2,512,128]{3,2,1,0:T(8,128)(2,1)S(1)}, f32[4,1,1024]{2,1,0:T(1,128)S(1)}, f32[8,128]{1,0:T(8,128)S(1)}) custom-call(bf16[2,4,2,512,512]{4,3,2,1,0:T(8,128)(2,1)S(1)} %get-tuple-element.137.refs_0_, ...), custom_call_target="tpu_custom_call" | custom-call | flops 17999998976 | bytes 1048576 | tf_op jit(solution)/shard_map/attend_backward/pallas_call | solution.py:59
  58.0 3.9 %collective-permute-done.5.refs_1_ = bf16[768,512]{1,0:T(8,128)(2,1)S(1)} collective-permute-done((bf16[768,512]{1,0:T(8,128)(2,1)S(1)}, bf16[768,512]{1,0:T(8,128)(2,1)S(1)}, u32[]{:S(2)}, u32[]{:S(2)}) %collective-permute-start.5) | collective-permute-done | bytes 786464 | tf_op jit(solution)/shard_map/ppermute | solution.py:590
  62.1 2.1 %collective-permute-start.6 = (bf16[384,512]{1,0:T(8,128)(2,1)S(1)}, bf16[384,512]{1,0:T(8,128)(2,1)S(1)}, u32[]{:S(2)}, u32[]{:S(2)}) collective-permute-start(bf16[384,512]{1,0:T(8,128)(2,1)S(1)} %get-tuple-element.165), channel_id=1, source_target_pairs={{0,4},{1,3},{2,6},{3,1},{4,0},{5,7},{6,2},{7,5},{8,12},{9,11},{10,... | collective-permute-start | bytes 1179656 | tf_op jit(solution)/shard_map/ppermute | solution.py:590
  64.2 6.0 %attend_backward.3 = (bf16[2,2,512,128]{3,2,1,0:T(8,128)(2,1)S(1)}, bf16[2,2,512,128]{3,2,1,0:T(8,128)(2,1)S(1)}, bf16[2,2,512,128]{3,2,1,0:T(8,128)(2,1)S(1)}, f32[4,1,1024]{2,1,0:T(1,128)S(1)}, f32[8,128]{1,0:T(8,128)S(1)}) custom-call(bf16[2,4,2,512,512]{4,3,2,1,0:T(8,128)(2,1)S(1)} %get-tuple-element.137.refs_0_, ...), custom_call_target="tpu_custom_call" | custom-call | flops 17999998976 | bytes 1048576 | tf_op jit(solution)/shard_map/attend_backward/pallas_call | solution.py:59
  70.4 4.1 %weight_grads.1 = (bf16[1536,512]{1,0:T(8,128)(2,1)S(1)}, bf16[1568,512]{1,0:T(8,128)(2,1)S(1)}, bf16[32,512]{1,0:T(8,128)(2,1)S(1)}, f32[8,128]{1,0:T(8,128)S(1)}) custom-call(bf16[2,512,512]{2,1,0:T(8,128)(2,1)S(1)} %get-tuple-element.157.refs_0_, bf16[2,2,512,128]{3,2,1,0:T(8,128)(2,1)S(1)} %get-tuple-element.147.refs_1_.refs_2_, ...), custom_call_target="tpu_custom_call" | custom-call | flops 8999999488 | bytes 1048576 | tf_op jit(solution)/shard_map/weight_grads/pallas_call | solution.py:59
  74.5 1.9 %collective-permute-start.8 = (bf16[192,512]{1,0:T(8,128)(2,1)S(1)}, bf16[192,512]{1,0:T(8,128)(2,1)S(1)}, u32[]{:S(2)}, u32[]{:S(2)}) collective-permute-start(bf16[192,512]{1,0:T(8,128)(2,1)S(1)} %get-tuple-element.172), channel_id=1, source_target_pairs={{0,8},{1,9},{2,10},{3,11},{4,12},{5,13},{6,14},{7,15},{8,0},{9,1},... | collective-permute-start | bytes 589832 | tf_op jit(solution)/shard_map/ppermute | solution.py:590
  76.4 3.7 %input_grad.1 = (bf16[2,256,512]{2,1,0:T(8,128)(2,1)S(1)}, bf16[2,256,512]{2,1,0:T(8,128)(2,1)S(1)}, f32[8,128]{1,0:T(8,128)S(1)}) custom-call(bf16[2,512,512]{2,1,0:T(8,128)(2,1)S(1)} %get-tuple-element.135.refs_0_, f32[2,512,512]{2,1,0:T(8,128)S(1)} %get-tuple-element.136.refs_1_, bf16[2,2,512,128]{3,2,1,0:T(8,128)(2,1)S(1)} %get-tuple-element.147.refs_1_.refs_2_, ...), custom_call_target="tpu_custom_call" | custom-call | flops 12000000000 | bytes 1048576 | tf_op jit(solution)/shard_map/input_grad/pallas_call | solution.py:59
  80.1 1.8 %collective-permute-done.8.refs_1_ = bf16[192,512]{1,0:T(8,128)(2,1)S(1)} collective-permute-done((bf16[192,512]{1,0:T(8,128)(2,1)S(1)}, bf16[192,512]{1,0:T(8,128)(2,1)S(1)}, u32[]{:S(2)}, u32[]{:S(2)}) %collective-permute-start.8) | collective-permute-done | bytes 196640 | tf_op jit(solution)/shard_map/ppermute | solution.py:590
  82.3 1.8 %collective-permute-start.12 = (bf16[800,512]{1,0:T(8,128)(2,1)S(1)}, bf16[800,512]{1,0:T(8,128)(2,1)S(1)}, u32[]{:S(2)}, u32[]{:S(2)}) collective-permute-start(bf16[800,512]{1,0:T(8,128)(2,1)S(1)} %get-tuple-element.182), channel_id=1, source_target_pairs={{0,4},{1,3},{2,6},{3,1},{4,0},{5,7},{6,2},{7,5},{8,12},{9,11},{10,... | collective-permute-start | bytes 2457608 | tf_op jit(solution)/shard_map/ppermute | solution.py:590
  84.1 2.6 %collective-permute-start.9 = (bf16[192,512]{1,0:T(8,128)(2,1)S(1)}, bf16[192,512]{1,0:T(8,128)(2,1)S(1)}, u32[]{:S(2)}, u32[]{:S(2)}) collective-permute-start(bf16[192,512]{1,0:T(8,128)(2,1)S(1)} %get-tuple-element.174.refs_0_), channel_id=1, source_target_pairs={{0,16},{1,17},{2,18},{3,19},{4,20},{5,21},{6,22},{7,23},{8,24},{9,... | collective-permute-start | bytes 589832 | tf_op jit(solution)/shard_map/ppermute | solution.py:590
  86.7 8.7 %collective-permute-done.9.refs_1_ = bf16[192,512]{1,0:T(8,128)(2,1)S(1)} collective-permute-done((bf16[192,512]{1,0:T(8,128)(2,1)S(1)}, bf16[192,512]{1,0:T(8,128)(2,1)S(1)}, u32[]{:S(2)}, u32[]{:S(2)}) %collective-permute-start.9) | collective-permute-done | bytes 196640 | tf_op jit(solution)/shard_map/ppermute | solution.py:590
  96.7 1.6 collective-permute-start.11
  98.3 5.3 %collective-permute-done.11.refs_1_ = bf16[192,512]{1,0:T(8,128)(2,1)S(1)} collective-permute-done((bf16[192,512]{1,0:T(8,128)(2,1)S(1)}, bf16[192,512]{1,0:T(8,128)(2,1)S(1)}, u32[]{:S(2)}, u32[]{:S(2)}) %collective-permute-start.11) | collective-permute-done | bytes 196640 | tf_op jit(solution)/shard_map/ppermute | solution.py:590
  104.1 1.6 %collective-permute-start.15 = (bf16[224,512]{1,0:T(8,128)(2,1)S(1)}, bf16[224,512]{1,0:T(8,128)(2,1)S(1)}, u32[]{:S(2)}, u32[]{:S(2)}) collective-permute-start(bf16[224,512]{1,0:T(8,128)(2,1)S(1)} %get-tuple-element.192), channel_id=1, source_target_pairs={{0,8},{1,9},{2,10},{3,11},{4,12},{5,13},{6,14},{7,15},{8,0},{9,1},... | collective-permute-start | bytes 688136 | tf_op jit(solution)/shard_map/ppermute | solution.py:590
  105.7 4.8 %collective-permute-done.15.refs_1_ = bf16[224,512]{1,0:T(8,128)(2,1)S(1)} collective-permute-done((bf16[224,512]{1,0:T(8,128)(2,1)S(1)}, bf16[224,512]{1,0:T(8,128)(2,1)S(1)}, u32[]{:S(2)}, u32[]{:S(2)}) %collective-permute-start.15) | collective-permute-done | bytes 229408 | tf_op jit(solution)/shard_map/ppermute | solution.py:590
  112.4 2.8 %collective-permute-start.17 = (bf16[224,512]{1,0:T(8,128)(2,1)S(1)}, bf16[224,512]{1,0:T(8,128)(2,1)S(1)}, u32[]{:S(2)}, u32[]{:S(2)}) collective-permute-start(bf16[224,512]{1,0:T(8,128)(2,1)S(1)} %get-tuple-element.198), channel_id=1, source_target_pairs={{0,16},{1,17},{2,18},{3,19},{4,20},{5,21},{6,22},{7,23},{8,24},{9,... | collective-permute-start | bytes 688136 | tf_op jit(solution)/shard_map/ppermute | solution.py:590
  115.2 8.0 %collective-permute-done.17.refs_1_ = bf16[224,512]{1,0:T(8,128)(2,1)S(1)} collective-permute-done((bf16[224,512]{1,0:T(8,128)(2,1)S(1)}, bf16[224,512]{1,0:T(8,128)(2,1)S(1)}, u32[]{:S(2)}, u32[]{:S(2)}) %collective-permute-start.17) | collective-permute-done | bytes 229408 | tf_op jit(solution)/shard_map/ppermute | solution.py:590
  125.2 5.8 %collective-permute-done.19.refs_1_ = bf16[192,512]{1,0:T(8,128)(2,1)S(1)} collective-permute-done((bf16[192,512]{1,0:T(8,128)(2,1)S(1)}, bf16[192,512]{1,0:T(8,128)(2,1)S(1)}, u32[]{:S(2)}, u32[]{:S(2)}) %collective-permute-start.19) | collective-permute-done | bytes 196640 | tf_op jit(solution)/shard_map/ppermute | solution.py:590
  131.0 1.7 %collective-permute-start.20 = (bf16[384,512]{1,0:T(8,128)(2,1)S(1)}, bf16[384,512]{1,0:T(8,128)(2,1)S(1)}, u32[]{:S(2)}, u32[]{:S(2)}) collective-permute-start(bf16[384,512]{1,0:T(8,128)(2,1)S(1)} %get-tuple-element.209.refs_0_), channel_id=1, source_target_pairs={{0,2},{1,5},{2,0},{3,7},{4,6},{5,1},{6,4},{7,3},{8,10},{9,13},{10,... | collective-permute-start | bytes 1179656 | tf_op jit(solution)/shard_map/ppermute | solution.py:590
  132.8 2.8 %feed_result.1 = (f32[2048,512]{1,0:T(8,128)}, f32[512,2048]{1,0:T(8,128)}, f32[8,128]{1,0:T(8,128)S(1)}) custom-call(bf16[1536,512]{1,0:T(8,128)(2,1)S(1)} %get-tuple-element.202.refs_0_, bf16[1536,512]{1,0:T(8,128)(2,1)S(1)} %collective-permute-done.18.refs_1_, f32[8,128]{1,0:T(8,128)S(1)} %get-tuple-element.205.refs_2_), custom_call_target="tpu_custom_call" | custom-call | flops 12000000000 | bytes 1048576 | tf_op jit(solution)/shard_map/feed_result/pallas_call | solution.py:59
  135.6 1.4 place.1
  137.0 1.9 %collective-permute-done.20.refs_1_ = bf16[384,512]{1,0:T(8,128)(2,1)S(1)} collective-permute-done((bf16[384,512]{1,0:T(8,128)(2,1)S(1)}, bf16[384,512]{1,0:T(8,128)(2,1)S(1)}, u32[]{:S(2)}, u32[]{:S(2)}) %collective-permute-start.20) | collective-permute-done | bytes 393248 | tf_op jit(solution)/shard_map/ppermute | solution.py:590
  138.9 1.6 collective-permute-start.21
  140.5 10.5 %collective-permute-done.21.refs_1_ = bf16[768,512]{1,0:T(8,128)(2,1)S(1)} collective-permute-done((bf16[768,512]{1,0:T(8,128)(2,1)S(1)}, bf16[768,512]{1,0:T(8,128)(2,1)S(1)}, u32[]{:S(2)}, u32[]{:S(2)}) %collective-permute-start.21) | collective-permute-done | bytes 786464 | tf_op jit(solution)/shard_map/ppermute | solution.py:590
  151.2 3.4 %collective-permute-done.22.refs_1_ = bf16[1568,512]{1,0:T(8,128)(2,1)S(1)} collective-permute-done((bf16[1568,512]{1,0:T(8,128)(2,1)S(1)}, bf16[1568,512]{1,0:T(8,128)(2,1)S(1)}, u32[]{:S(2)}, u32[]{:S(2)}) %collective-permute-start.22) | collective-permute-done | bytes 1605664 | tf_op jit(solution)/shard_map/ppermute | solution.py:590
  154.6 3.4 %rest_result.1 = (f32[2048,512]{1,0:T(8,128)}, f32[512,2048]{1,0:T(8,128)}, f32[512,512]{1,0:T(8,128)}, f32[512,512]{1,0:T(8,128)}, f32[512,512]{1,0:T(8,128)}, ...) custom-call(bf16[1568,512]{1,0:T(8,128)(2,1)S(1)} %get-tuple-element, ...), custom_call_target="tpu_custom_call", output_to_operand_aliasing={{0}: (2, {}), {1}: (3, {})} | custom-call | flops 8999999488 | bytes 1048576 | tf_op jit(solution)/shard_map/rest_result/pallas_call | solution.py:59
  (56 shorter events, 10.6 us)
Async XLA Ops:
  0.6 0.7 copy-start
  1.3 0.7 copy-start.1
  3.7 3.3 %collective-permute-start.1 = (bf16[2,256,512]{2,1,0:T(8,128)(2,1)S(1)}, bf16[2,256,512]{2,1,0:T(8,128)(2,1)S(1)}, u32[]{:S(2)}, u32[]{:S(2)}) collective-permute-start(bf16[2,256,512]{2,1,0:T(8,128)(2,1)S(1)} %get-tuple-element.122), channel_id=1, source_target_pairs={{0,1},{1,0},{2,3},{3,2},{4,5},{5,4},{6,7},{7,6},{8,9},{9,8},{10,11... | collective-permute-start | bytes 1572872 | tf_op jit(solution)/shard_map/ppermute | solution.py:659
  4.2 2.6 %copy-start.5 = (f32[32,8]{0,1:T(8,128)S(1)}, f32[32,8]{0,1:T(8,128)}, u32[]{:S(2)}) copy-start(f32[32,8]{0,1:T(8,128)} %param.27) | copy-start | bytes 3076
  4.2 2.8 %copy-start.2 = (f32[512]{0:T(512)S(1)}, f32[512]{0:T(512)}, u32[]{:S(2)}) copy-start(f32[512]{0:T(512)} %param.24) | copy-start | bytes 6148
  4.2 2.8 %copy-start.3 = (f32[512]{0:T(512)S(1)}, f32[512]{0:T(512)}, u32[]{:S(2)}) copy-start(f32[512]{0:T(512)} %param.19) | copy-start | bytes 6148
  4.2 2.8 %copy-start.4 = (s32[2,1]{0,1:T(1,128)S(1)}, s32[2,1]{0,1:T(1,128)}, u32[]{:S(2)}) copy-start(s32[2,1]{0,1:T(1,128)} %param.18) | copy-start | bytes 28
  4.2 2.8 %collective-permute-start.2 = (s32[2,2,256]{2,1,0:T(2,128)S(1)}, s32[2,2,256]{2,1,0:T(2,128)S(1)}, u32[]{:S(2)}, u32[]{:S(2)}) collective-permute-start(s32[2,2,256]{2,1,0:T(2,128)S(1)} %get-tuple-element.124), channel_id=1, source_target_pairs={{0,1},{1,0},{2,3},{3,2},{4,5},{5,4},{6,7},{7,6},{8,9},{9,8},{10,11... | collective-permute-start | bytes 12296 | tf_op jit(solution)/shard_map/ppermute | solution.py:659
  6.3 17.2 %collective-permute-start = (bf16[2,256,512]{2,1,0:T(8,128)(2,1)S(1)}, bf16[2,256,512]{2,1,0:T(8,128)(2,1)S(1)}, u32[]{:S(2)}, u32[]{:S(2)}) collective-permute-start(bf16[2,256,512]{2,1,0:T(8,128)(2,1)S(1)} %get-tuple-element.120), channel_id=1, source_target_pairs={{0,1},{1,0},{2,3},{3,2},{4,5},{5,4},{6,7},{7,6},{8,9},{9,8},{10,11... | collective-permute-start | bytes 1572872 | tf_op jit(solution)/shard_map/ppermute | solution.py:659
  40.0 8.5 %collective-permute-start.4 = (bf16[1536,512]{1,0:T(8,128)(2,1)S(1)}, bf16[1536,512]{1,0:T(8,128)(2,1)S(1)}, u32[]{:S(2)}, u32[]{:S(2)}) collective-permute-start(bf16[1536,512]{1,0:T(8,128)(2,1)S(1)} %get-tuple-element.144), channel_id=1, source_target_pairs={{0,1},{1,0},{2,3},{3,2},{4,5},{5,4},{6,7},{7,6},{8,9},{9,8},{10,11... | collective-permute-start | bytes 4718600 | tf_op jit(solution)/shard_map/ppermute | solution.py:590
  48.9 13.0 %collective-permute-start.5 = (bf16[768,512]{1,0:T(8,128)(2,1)S(1)}, bf16[768,512]{1,0:T(8,128)(2,1)S(1)}, u32[]{:S(2)}, u32[]{:S(2)}) collective-permute-start(bf16[768,512]{1,0:T(8,128)(2,1)S(1)} %get-tuple-element.149), channel_id=1, source_target_pairs={{0,2},{1,5},{2,0},{3,7},{4,6},{5,1},{6,4},{7,3},{8,10},{9,13},{10,... | collective-permute-start | bytes 2359304 | tf_op jit(solution)/shard_map/ppermute | solution.py:590
  62.1 8.1 %collective-permute-start.6 = (bf16[384,512]{1,0:T(8,128)(2,1)S(1)}, bf16[384,512]{1,0:T(8,128)(2,1)S(1)}, u32[]{:S(2)}, u32[]{:S(2)}) collective-permute-start(bf16[384,512]{1,0:T(8,128)(2,1)S(1)} %get-tuple-element.165), channel_id=1, source_target_pairs={{0,4},{1,3},{2,6},{3,1},{4,0},{5,7},{6,2},{7,5},{8,12},{9,11},{10,... | collective-permute-start | bytes 1179656 | tf_op jit(solution)/shard_map/ppermute | solution.py:590
  74.4 7.5 %collective-permute-start.10 = (bf16[1568,512]{1,0:T(8,128)(2,1)S(1)}, bf16[1568,512]{1,0:T(8,128)(2,1)S(1)}, u32[]{:S(2)}, u32[]{:S(2)}) collective-permute-start(bf16[1568,512]{1,0:T(8,128)(2,1)S(1)} %get-tuple-element.176), channel_id=1, source_target_pairs={{0,1},{1,0},{2,3},{3,2},{4,5},{5,4},{6,7},{7,6},{8,9},{9,8},{10,11... | collective-permute-start | bytes 4816904 | tf_op jit(solution)/shard_map/ppermute | solution.py:590
  74.5 7.4 %collective-permute-start.8 = (bf16[192,512]{1,0:T(8,128)(2,1)S(1)}, bf16[192,512]{1,0:T(8,128)(2,1)S(1)}, u32[]{:S(2)}, u32[]{:S(2)}) collective-permute-start(bf16[192,512]{1,0:T(8,128)(2,1)S(1)} %get-tuple-element.172), channel_id=1, source_target_pairs={{0,8},{1,9},{2,10},{3,11},{4,12},{5,13},{6,14},{7,15},{8,0},{9,1},... | collective-permute-start | bytes 589832 | tf_op jit(solution)/shard_map/ppermute | solution.py:590
  82.3 13.1 %collective-permute-start.12 = (bf16[800,512]{1,0:T(8,128)(2,1)S(1)}, bf16[800,512]{1,0:T(8,128)(2,1)S(1)}, u32[]{:S(2)}, u32[]{:S(2)}) collective-permute-start(bf16[800,512]{1,0:T(8,128)(2,1)S(1)} %get-tuple-element.182), channel_id=1, source_target_pairs={{0,4},{1,3},{2,6},{3,1},{4,0},{5,7},{6,2},{7,5},{8,12},{9,11},{10,... | collective-permute-start | bytes 2457608 | tf_op jit(solution)/shard_map/ppermute | solution.py:590
  84.1 11.3 %collective-permute-start.9 = (bf16[192,512]{1,0:T(8,128)(2,1)S(1)}, bf16[192,512]{1,0:T(8,128)(2,1)S(1)}, u32[]{:S(2)}, u32[]{:S(2)}) collective-permute-start(bf16[192,512]{1,0:T(8,128)(2,1)S(1)} %get-tuple-element.174.refs_0_), channel_id=1, source_target_pairs={{0,16},{1,17},{2,18},{3,19},{4,20},{5,21},{6,22},{7,23},{8,24},{9,... | collective-permute-start | bytes 589832 | tf_op jit(solution)/shard_map/ppermute | solution.py:590
  95.6 8.3 %collective-permute-start.14 = (bf16[416,512]{1,0:T(8,128)(2,1)S(1)}, bf16[416,512]{1,0:T(8,128)(2,1)S(1)}, u32[]{:S(2)}, u32[]{:S(2)}) collective-permute-start(bf16[416,512]{1,0:T(8,128)(2,1)S(1)} %get-tuple-element.188), channel_id=1, source_target_pairs={{0,2},{1,5},{2,0},{3,7},{4,6},{5,1},{6,4},{7,3},{8,10},{9,13},{10,... | collective-permute-start | bytes 1277960 | tf_op jit(solution)/shard_map/ppermute | solution.py:590
  96.7 6.8 %collective-permute-start.11 = (bf16[192,512]{1,0:T(8,128)(2,1)S(1)}, bf16[192,512]{1,0:T(8,128)(2,1)S(1)}, u32[]{:S(2)}, u32[]{:S(2)}) collective-permute-start(bf16[192,512]{1,0:T(8,128)(2,1)S(1)} %get-tuple-element.180.refs_0_), channel_id=1, source_target_pairs={{0,8},{1,9},{2,10},{3,11},{4,12},{5,13},{6,14},{7,15},{8,0},{9,1},... | collective-permute-start | bytes 589832 | tf_op jit(solution)/shard_map/ppermute | solution.py:590
  103.5 7.8 %collective-permute-start.13 = (bf16[384,512]{1,0:T(8,128)(2,1)S(1)}, bf16[384,512]{1,0:T(8,128)(2,1)S(1)}, u32[]{:S(2)}, u32[]{:S(2)}) collective-permute-start(bf16[384,512]{1,0:T(8,128)(2,1)S(1)} %get-tuple-element.186.refs_0_), channel_id=1, source_target_pairs={{0,4},{1,3},{2,6},{3,1},{4,0},{5,7},{6,2},{7,5},{8,12},{9,11},{10,... | collective-permute-start | bytes 1179656 | tf_op jit(solution)/shard_map/ppermute | solution.py:590
  104.1 6.4 %collective-permute-start.15 = (bf16[224,512]{1,0:T(8,128)(2,1)S(1)}, bf16[224,512]{1,0:T(8,128)(2,1)S(1)}, u32[]{:S(2)}, u32[]{:S(2)}) collective-permute-start(bf16[224,512]{1,0:T(8,128)(2,1)S(1)} %get-tuple-element.192), channel_id=1, source_target_pairs={{0,8},{1,9},{2,10},{3,11},{4,12},{5,13},{6,14},{7,15},{8,0},{9,1},... | collective-permute-start | bytes 688136 | tf_op jit(solution)/shard_map/ppermute | solution.py:590
  111.4 12.1 %collective-permute-start.16 = (bf16[768,512]{1,0:T(8,128)(2,1)S(1)}, bf16[768,512]{1,0:T(8,128)(2,1)S(1)}, u32[]{:S(2)}, u32[]{:S(2)}) collective-permute-start(bf16[768,512]{1,0:T(8,128)(2,1)S(1)} %get-tuple-element.196.refs_0_), channel_id=1, source_target_pairs={{0,2},{1,5},{2,0},{3,7},{4,6},{5,1},{6,4},{7,3},{8,10},{9,13},{10,... | collective-permute-start | bytes 2359304 | tf_op jit(solution)/shard_map/ppermute | solution.py:590
  112.4 10.8 %collective-permute-start.17 = (bf16[224,512]{1,0:T(8,128)(2,1)S(1)}, bf16[224,512]{1,0:T(8,128)(2,1)S(1)}, u32[]{:S(2)}, u32[]{:S(2)}) collective-permute-start(bf16[224,512]{1,0:T(8,128)(2,1)S(1)} %get-tuple-element.198), channel_id=1, source_target_pairs={{0,16},{1,17},{2,18},{3,19},{4,20},{5,21},{6,22},{7,23},{8,24},{9,... | collective-permute-start | bytes 688136 | tf_op jit(solution)/shard_map/ppermute | solution.py:590
  123.6 9.2 %collective-permute-start.18 = (bf16[1536,512]{1,0:T(8,128)(2,1)S(1)}, bf16[1536,512]{1,0:T(8,128)(2,1)S(1)}, u32[]{:S(2)}, u32[]{:S(2)}) collective-permute-start(bf16[1536,512]{1,0:T(8,128)(2,1)S(1)} %get-tuple-element.202.refs_0_), channel_id=1, source_target_pairs={{0,1},{1,0},{2,3},{3,2},{4,5},{5,4},{6,7},{7,6},{8,9},{9,8},{10,11... | collective-permute-start | bytes 4718600 | tf_op jit(solution)/shard_map/ppermute | solution.py:590
  123.7 7.3 %collective-permute-start.19 = (bf16[192,512]{1,0:T(8,128)(2,1)S(1)}, bf16[192,512]{1,0:T(8,128)(2,1)S(1)}, u32[]{:S(2)}, u32[]{:S(2)}) collective-permute-start(bf16[192,512]{1,0:T(8,128)(2,1)S(1)} %get-tuple-element.203.refs_0_), channel_id=1, source_target_pairs={{0,8},{1,9},{2,10},{3,11},{4,12},{5,13},{6,14},{7,15},{8,0},{9,1},... | collective-permute-start | bytes 589832 | tf_op jit(solution)/shard_map/ppermute | solution.py:590
  124.7 10.9 %collective-permute-start.3 = (bf16[2,256,512]{2,1,0:T(8,128)(2,1)S(1)}, bf16[2,256,512]{2,1,0:T(8,128)(2,1)S(1)}, u32[]{:S(2)}, u32[]{:S(2)}) collective-permute-start(bf16[2,256,512]{2,1,0:T(8,128)(2,1)S(1)} %get-tuple-element.134), channel_id=1, source_target_pairs={{0,1},{1,0},{2,3},{3,2},{4,5},{5,4},{6,7},{7,6},{8,9},{9,8},{10,11... | collective-permute-start | bytes 1572872 | tf_op jit(solution)/shard_map/ppermute | solution.py:659
  124.9 10.7 %collective-permute-start.7 = (bf16[2,256,512]{2,1,0:T(8,128)(2,1)S(1)}, bf16[2,256,512]{2,1,0:T(8,128)(2,1)S(1)}, u32[]{:S(2)}, u32[]{:S(2)}) collective-permute-start(bf16[2,256,512]{2,1,0:T(8,128)(2,1)S(1)} %get-tuple-element.170), channel_id=1, source_target_pairs={{0,1},{1,0},{2,3},{3,2},{4,5},{5,4},{6,7},{7,6},{8,9},{9,8},{10,11... | collective-permute-start | bytes 1572872 | tf_op jit(solution)/shard_map/ppermute | solution.py:659
  131.0 7.8 %collective-permute-start.20 = (bf16[384,512]{1,0:T(8,128)(2,1)S(1)}, bf16[384,512]{1,0:T(8,128)(2,1)S(1)}, u32[]{:S(2)}, u32[]{:S(2)}) collective-permute-start(bf16[384,512]{1,0:T(8,128)(2,1)S(1)} %get-tuple-element.209.refs_0_), channel_id=1, source_target_pairs={{0,2},{1,5},{2,0},{3,7},{4,6},{5,1},{6,4},{7,3},{8,10},{9,13},{10,... | collective-permute-start | bytes 1179656 | tf_op jit(solution)/shard_map/ppermute | solution.py:590
  138.9 12.1 %collective-permute-start.21 = (bf16[768,512]{1,0:T(8,128)(2,1)S(1)}, bf16[768,512]{1,0:T(8,128)(2,1)S(1)}, u32[]{:S(2)}, u32[]{:S(2)}) collective-permute-start(bf16[768,512]{1,0:T(8,128)(2,1)S(1)} %get-tuple-element.211.refs_0_), channel_id=1, source_target_pairs={{0,4},{1,3},{2,6},{3,1},{4,0},{5,7},{6,2},{7,5},{8,12},{9,11},{10,... | collective-permute-start | bytes 2359304 | tf_op jit(solution)/shard_map/ppermute | solution.py:590
  151.1 3.5 %collective-permute-start.22 = (bf16[1568,512]{1,0:T(8,128)(2,1)S(1)}, bf16[1568,512]{1,0:T(8,128)(2,1)S(1)}, u32[]{:S(2)}, u32[]{:S(2)}) collective-permute-start(bf16[1568,512]{1,0:T(8,128)(2,1)S(1)} %get-tuple-element.214.refs_0_), channel_id=1, source_target_pairs={{0,1},{1,0},{2,3},{3,2},{4,5},{5,4},{6,7},{7,6},{8,9},{9,8},{10,11... | collective-permute-start | bytes 4816904 | tf_op jit(solution)/shard_map/ppermute | solution.py:590

commit v2 on v1

--- a/solution.py
+++ b/solution.py
@@ -142,15 +142,18 @@
     return w_in.at[:, pl.ds(start, width)], w_down.at[pl.ds(start, width), :]
 
 
-def pick_kernel(who, tok, seg, pad, tok_send, marks_own, marks_send, sems):
+def pick_kernel(who, tok, seg, pad, tok_send, marks_own, marks_send, near, sems):
     c = who[0]
     rows = tok.shape[0]
     copies = [pltpu.make_async_copy(tok.at[m, 1 - c], tok_send.at[m], sems.at[m]) for m in range(rows)]
-    for copy in copies:
+    marked = [pltpu.make_async_copy(marks, near.at[i], sems.at[rows + i]) for i, marks in enumerate((seg, pad))]
+    for copy in copies + marked:
         copy.start()
-    for kind, marks in enumerate((seg, pad)):
+    for copy in marked:
+        copy.wait()
+    for kind in range(2):
         for m in range(rows):
-            first, second = marks[m, pl.ds(0, 1)], marks[m, pl.ds(1, 1)]
+            first, second = near[kind, m, pl.ds(0, 1)], near[kind, m, pl.ds(1, 1)]
             marks_own[kind, pl.ds(m, 1)] = jnp.where(c == 0, first, second)
             marks_send[kind, pl.ds(m, 1)] = jnp.where(c == 0, second, first)
     for copy in copies:
@@ -516,26 +519,41 @@
         copy.wait()
 
 
-def rest_result_kernel(
-    who, own, got, down_in, in_in, down_out, in_out, o_out, q_out, k_out, v_out, ga_out, gf_out, table_out, made, sems
-):
-    width = own.shape[1]
-    last = slice(down_out.shape[0] - width, down_out.shape[0])
-    targets = (down_out.at[last, :], in_out.at[:, last], o_out, q_out, k_out, v_out)
+def rest_half_kernel(theirs, who, part, *refs):
+    core = 1 - who[0] if theirs else who[0]
+    refs = refs[7:] if theirs else refs[2:]
+    down_out, in_out, o_out, q_out, k_out, v_out = refs[:6]
+    made, sems = refs[-2:]
+    width = part.shape[1]
+    half = width // 2
+    start = lambda base: pl.ds(pl.multiple_of(base + core * half, half), half)
+    last = down_out.shape[0] - width
+    targets = [down_out.at[start(last), :], in_out.at[start(0), last : last + width]]
+    targets += [out.at[start(0), :] for out in (o_out, q_out, k_out, v_out)]
+    places = 1 << (LEVELS - 1)
+    count = half // places
+    mask = jnp.where(core == 0, who[1], who[2])
     copies = []
     for i, target in enumerate(targets):
-        fill_block(made.at[i], i, 6, who, own, got)
+        for k in range(places):
+            first = pl.multiple_of((jnp.bitwise_xor(k, mask) * 6 + i) * count, count)
+            made[i, k * count : (k + 1) * count, :] = part[pl.ds(first, count), :].astype(F32)
         copies.append(pltpu.make_async_copy(made.at[i], target, sems.at[i]))
         copies[-1].start()
+    for copy in copies:
+        copy.wait()
+
+
+def other_result_kernel(who, part, *refs):
+    own, outs = refs[6], refs[7:13]
+    ga_out, gf_out, table_out, made, sems = refs[13:]
+    rest_half_kernel(True, who, part, *refs[:7], *outs, made, sems)
     tail = own.shape[0] - SMALL
-    small = jnp.where(who[0] == 0, own[tail:, :].astype(F32), got[tail:, :].astype(F32))
+    small = jnp.where(who[0] == 0, own[tail:, :].astype(F32), part[tail:, :].astype(F32))
     small = small[: SMALL // 2] + small[SMALL // 2 :]
     ga_out[...] = small[:1]
     gf_out[...] = small[1:2]
-    table = jnp.concatenate([small[8:, :TILE], jnp.zeros((TILE - 8, TILE), F32)], 0).T
-    table_out[...] = table[: table_out.shape[0], : table_out.shape[1]]
-    for copy in copies:
-        copy.wait()
+    table_out[...] = small[8:, : table_out.shape[1]]
 
 
 def land_kernel(has_small, then, *refs):
@@ -657,9 +675,9 @@
 
     who = [where_am_i(order) for order in orders]
     swap = lambda a: lax.ppermute(a, ("dp", "seq"), swap_pairs(dp, None))
-    tokens, cotangent, w_query, w_key, w_value, w_out, w_in, w_down = (
+    tokens, cotangent, segments, pad_mask, w_query, w_key, w_value, w_out, w_in, w_down = (
         pltpu.with_memory_space_constraint(array, pltpu.HBM)
-        for array in (tokens, cotangent, w_query, w_key, w_value, w_out, w_in, w_down)
+        for array in (tokens, cotangent, segments, pad_mask, w_query, w_key, w_value, w_out, w_in, w_down)
     )
     table = jnp.broadcast_to(position_bias_table[:, :, None], (bucket_count, heads, 1))
     gain, fgain = attend_gain.reshape(1, width), forward_gain.reshape(1, width)
@@ -675,8 +693,8 @@
     call = calls.call
 
     tok_send, marks_own, marks_send = call(
-        pick_kernel, "pick", 1, (tokens, segments, pad_mask), [far(), whole(), whole()],
-        (row_half, marked, marked), scratch=[dma((rows,))], who=who[0],
+        pick_kernel, "pick", 1, (tokens, segments, pad_mask), [far()] * 3,
+        (row_half, marked, marked), scratch=[vm((2, rows, slots, half), jnp.int32), dma((rows + 2,))], who=who[0],
     )
     tok_got, marks_got = swap(tok_send), swap(marks_send)
     tok_own, cot_own, cot_send = call(
@@ -795,19 +813,20 @@
                 place_kernel, "place", 1, (out_own, out_got, in_own, in_got), [whole()] * 4,
                 (all_rows, all_rows), out_specs=[far(), far()], scratch=[dma((4 * rows,))], who=who[0],
             )
-    grad_down, grad_in, grad_out, grad_query, grad_key, grad_value, ga, gf, grad_table = call(
-        rest_result_kernel, "rest_result", 3,
-        (*c_piece.done(), grad_down, grad_in), [whole()] * 2 + [far()] * 2,
-        (
-            sds((ff, width), F32), sds((width, ff), F32), square, square, square, square,
-            sds((1, width), F32), sds((1, width), F32), sds((bucket_count, heads), F32),
-        ),
+    own, got = c_piece.done()
+    shapes = (sds((ff, width), F32), sds((width, ff), F32), square, square, square, square)
+    result_scratch = [vm((6, width // 2, width), F32), dma((6,))]
+    results = call(
+        functools.partial(rest_half_kernel, False), "own_result", 2, (own, grad_down, grad_in), [whole()] + [far()] * 2,
+        shapes, out_specs=[far()] * 6, scratch=result_scratch, vmem=VMEM[7], aliases={1: 0, 2: 1}, who=who[1],
+    )
+    *results, ga, gf, grad_table = call(
+        functools.partial(other_result_kernel), "other_result", 2, (got, *results, own), [whole()] + [far()] * 6 + [whole()],
+        (*shapes, sds((1, width), F32), sds((1, width), F32), sds((heads, bucket_count), F32)),
         out_specs=[far()] * 6 + [whole()] * 3,
-        scratch=[vm((6, width, width), F32), dma((6,))],
-        vmem=VMEM[7],
-        aliases={2: 0, 3: 1},
-        who=who[1],
-    )
+        scratch=result_scratch, vmem=VMEM[7], aliases={1 + n: n for n in range(6)}, who=who[1],
+    )
+    grad_down, grad_in, grad_out, grad_query, grad_key, grad_value = results
 
     return (
         output,
@@ -820,7 +839,7 @@
         gf.reshape(width),
         grad_in,
         grad_down,
-        grad_table,
+        grad_table.T,
     )
 
 

time: 159 us -> 156 us (0.981)
  local copies, waits for them, and re-layouts: 2.18 us -> 0.16 us
  waiting for transfers between devices: 55.1 us -> 53.3 us
    unnamed x13 -> x8, local copies, waits for them, and re-layouts: 2.04 us -> 0.01 us
    ppermute x18, waiting for transfers between devices: 55.1 us -> 53.3 us  [fly(): lax.ppermute(self.send, ('dp', 'seq'), swap_pairs(self.dp, self.steps[0][...]
    pallas_call x28 -> x29, Pallas kernels: 74.4 us -> 75.1 us  [call(): pl.pallas_call(body, grid=(grid,), in_specs=list(in_specs) + [whole()] *...]
  transfers between devices with their start and end apart: 23 -> 23, of which waited for: 12 -> 12; matrix products, arithmetic and copies ran while one was open for 0% -> 0% of each run, Pallas kernels for 30% -> 31%
where the time goes in v2:
time: 156 us
  Pallas kernels  75.1 us (48%)
  waiting for transfers between devices  53.3 us (34%)
  starting transfers between devices  26.1 us (17%)
    pallas_call x29, Pallas kernels, call(): pl.pallas_call(body, grid=(grid,), in_specs=list(in_specs) + [whole()] *...  75.1 us
    ppermute x18, waiting for transfers between devices, fly(): lax.ppermute(self.send, ('dp', 'seq'), swap_pairs(self.dp, self.steps[0][...  53.3 us
    ppermute x18, starting transfers between devices, fly(): lax.ppermute(self.send, ('dp', 'seq'), swap_pairs(self.dp, self.steps[0][...  24.4 us
  transfers between devices with their start and end apart: 23, of which 12 were waited for; matrix products, arithmetic and copies ran while one was open for 0% of the time, Pallas kernels for 31%

profile of v2, /device:TPU:0, one launch (start us, length us, event | category | flops | bytes accessed | tf_op | source)
XLA Modules:
  0.0 155.8 jit_solution(17343585921705406339)
XLA Ops:
  0.6 1.7 %pick.1 = (bf16[2,256,512]{2,1,0:T(8,128)(2,1)S(1)}, s32[2,2,256]{2,1,0:T(2,128)S(1)}, s32[2,2,256]{2,1,0:T(2,128)S(1)}, f32[8,128]{1,0:T(8,128)}) custom-call(bf16[2,2,256,512]{3,2,1,0:T(8,128)(2,1)} %refs_0_.3, s32[2,2,256]{2,1,0:T(2,128)} %refs_1_.3, s32[2,2,256]{2,1,0:T(2,128)} %refs_2_.1), custom_call_target="tpu_custom_call" | custom-call | flops 3000000000 | bytes 1048576 | tf_op jit(solution)/shard_map/pick/pallas_call | solution.py:59
  3.0 2.0 %pick_rest.1 = (bf16[2,256,512]{2,1,0:T(8,128)(2,1)S(1)}, bf16[2,256,512]{2,1,0:T(8,128)(2,1)S(1)}, bf16[2,256,512]{2,1,0:T(8,128)(2,1)S(1)}, f32[8,128]{1,0:T(8,128)}) custom-call(bf16[2,2,256,512]{3,2,1,0:T(8,128)(2,1)} %refs_0_.3, bf16[2,2,256,512]{3,2,1,0:T(8,128)(2,1)} %refs_1_.2), custom_call_target="tpu_custom_call" | custom-call | flops 3000000000 | bytes 1048576 | tf_op jit(solution)/shard_map/pick_rest/pallas_call | solution.py:59
  5.7 16.4 %attend_forward.1 = (bf16[2,512,512]{2,1,0:T(8,128)(2,1)S(1)}, bf16[2,512,512]{2,1,0:T(8,128)(2,1)S(1)}, bf16[2,4,512,128]{3,2,1,0:T(8,128)(2,1)S(1)}, bf16[2,4,...) custom-call(s32[2]{0:T(128)S(1)} %bitcast.12, ...), custom_call_target="tpu_custom_call" | custom-call | flops 41999998976 | bytes 1048576 | tf_op jit(solution)/shard_map/attend_forward/pallas_call | solution.py:59
  22.1 16.6 %feed_first.1 = (bf16[2,512,512]{2,1,0:T(8,128)(2,1)S(1)}, bf16[2,512,512]{2,1,0:T(8,128)(2,1)S(1)}, f32[2,512,512]{2,1,0:T(8,128)S(1)}, f32[2,512,512]{2,1,0:T(...) custom-call(bf16[2,256,512]{2,1,0:T(8,128)(2,1)S(1)} %get-tuple-element.126.refs_0_, ...), custom_call_target="tpu_custom_call" | custom-call | flops 44999999488 | bytes 1048576 | tf_op jit(solution)/shard_map/feed_first/pallas_call | solution.py:59
  38.8 8.4 %feed_third.1 = (f32[2,512,512]{2,1,0:T(8,128)S(1)}, f32[2,512,512]{2,1,0:T(8,128)S(1)}, bf16[2,256,512]{2,1,0:T(8,128)(2,1)S(1)}, bf16[2,256,512]{2,1,0:T(8,128...) custom-call(bf16[2,512,512]{2,1,0:T(8,128)(2,1)S(1)} %get-tuple-elem, ...), custom_call_target="tpu_custom_call", output_to_operand_aliasing={{0}: (2, {}), {1}: (3, {})} | custom-call | flops 24000000000 | bytes 1048576 | tf_op jit(solution)/shard_map/feed_third/pallas_call | solution.py:59
  47.6 3.0 %collective-permute-start.5 = (bf16[768,512]{1,0:T(8,128)(2,1)S(1)}, bf16[768,512]{1,0:T(8,128)(2,1)S(1)}, u32[]{:S(2)}, u32[]{:S(2)}) collective-permute-start(bf16[768,512]{1,0:T(8,128)(2,1)S(1)} %get-tuple-element.156), channel_id=1, source_target_pairs={{0,2},{1,5},{2,0},{3,7},{4,6},{5,1},{6,4},{7,3},{8,10},{9,13},{10,... | collective-permute-start | bytes 2359304 | tf_op jit(solution)/shard_map/ppermute | solution.py:608
  50.6 6.0 %attend_backward.2 = (bf16[2,2,512,128]{3,2,1,0:T(8,128)(2,1)S(1)}, bf16[2,2,512,128]{3,2,1,0:T(8,128)(2,1)S(1)}, bf16[2,2,512,128]{3,2,1,0:T(8,128)(2,1)S(1)}, f32[4,1,1024]{2,1,0:T(1,128)S(1)}, f32[8,128]{1,0:T(8,128)S(1)}) custom-call(bf16[2,4,2,512,512]{4,3,2,1,0:T(8,128)(2,1)S(1)} %get-tuple-element.144.refs_0_, ...), custom_call_target="tpu_custom_call" | custom-call | flops 17999998976 | bytes 1048576 | tf_op jit(solution)/shard_map/attend_backward/pallas_call | solution.py:59
  56.6 3.9 %collective-permute-done.5.refs_1_ = bf16[768,512]{1,0:T(8,128)(2,1)S(1)} collective-permute-done((bf16[768,512]{1,0:T(8,128)(2,1)S(1)}, bf16[768,512]{1,0:T(8,128)(2,1)S(1)}, u32[]{:S(2)}, u32[]{:S(2)}) %collective-permute-start.5) | collective-permute-done | bytes 786464 | tf_op jit(solution)/shard_map/ppermute | solution.py:608
  60.8 2.1 %collective-permute-start.6 = (bf16[384,512]{1,0:T(8,128)(2,1)S(1)}, bf16[384,512]{1,0:T(8,128)(2,1)S(1)}, u32[]{:S(2)}, u32[]{:S(2)}) collective-permute-start(bf16[384,512]{1,0:T(8,128)(2,1)S(1)} %get-tuple-element.172), channel_id=1, source_target_pairs={{0,4},{1,3},{2,6},{3,1},{4,0},{5,7},{6,2},{7,5},{8,12},{9,11},{10,... | collective-permute-start | bytes 1179656 | tf_op jit(solution)/shard_map/ppermute | solution.py:608
  62.9 6.0 %attend_backward.3 = (bf16[2,2,512,128]{3,2,1,0:T(8,128)(2,1)S(1)}, bf16[2,2,512,128]{3,2,1,0:T(8,128)(2,1)S(1)}, bf16[2,2,512,128]{3,2,1,0:T(8,128)(2,1)S(1)}, f32[4,1,1024]{2,1,0:T(1,128)S(1)}, f32[8,128]{1,0:T(8,128)S(1)}) custom-call(bf16[2,4,2,512,512]{4,3,2,1,0:T(8,128)(2,1)S(1)} %get-tuple-element.144.refs_0_, ...), custom_call_target="tpu_custom_call" | custom-call | flops 17999998976 | bytes 1048576 | tf_op jit(solution)/shard_map/attend_backward/pallas_call | solution.py:59
  69.0 4.1 %weight_grads.1 = (bf16[1536,512]{1,0:T(8,128)(2,1)S(1)}, bf16[1568,512]{1,0:T(8,128)(2,1)S(1)}, bf16[32,512]{1,0:T(8,128)(2,1)S(1)}, f32[8,128]{1,0:T(8,128)S(1)}) custom-call(bf16[2,512,512]{2,1,0:T(8,128)(2,1)S(1)} %get-tuple-element.164.refs_0_, bf16[2,2,512,128]{3,2,1,0:T(8,128)(2,1)S(1)} %get-tuple-element.154.refs_1_.refs_2_, ...), custom_call_target="tpu_custom_call" | custom-call | flops 8999999488 | bytes 1048576 | tf_op jit(solution)/shard_map/weight_grads/pallas_call | solution.py:59
  73.2 1.9 %collective-permute-start.8 = (bf16[192,512]{1,0:T(8,128)(2,1)S(1)}, bf16[192,512]{1,0:T(8,128)(2,1)S(1)}, u32[]{:S(2)}, u32[]{:S(2)}) collective-permute-start(bf16[192,512]{1,0:T(8,128)(2,1)S(1)} %get-tuple-element.179), channel_id=1, source_target_pairs={{0,8},{1,9},{2,10},{3,11},{4,12},{5,13},{6,14},{7,15},{8,0},{9,1},... | collective-permute-start | bytes 589832 | tf_op jit(solution)/shard_map/ppermute | solution.py:608
  75.0 3.7 %input_grad.1 = (bf16[2,256,512]{2,1,0:T(8,128)(2,1)S(1)}, bf16[2,256,512]{2,1,0:T(8,128)(2,1)S(1)}, f32[8,128]{1,0:T(8,128)S(1)}) custom-call(bf16[2,512,512]{2,1,0:T(8,128)(2,1)S(1)} %get-tuple-element.142.refs_0_, f32[2,512,512]{2,1,0:T(8,128)S(1)} %get-tuple-element.143.refs_1_, bf16[2,2,512,128]{3,2,1,0:T(8,128)(2,1)S(1)} %get-tuple-element.154.refs_1_.refs_2_, ...), custom_call_target="tpu_custom_call" | custom-call | flops 12000000000 | bytes 1048576 | tf_op jit(solution)/shard_map/input_grad/pallas_call | solution.py:59
  78.7 1.8 %collective-permute-done.8.refs_1_ = bf16[192,512]{1,0:T(8,128)(2,1)S(1)} collective-permute-done((bf16[192,512]{1,0:T(8,128)(2,1)S(1)}, bf16[192,512]{1,0:T(8,128)(2,1)S(1)}, u32[]{:S(2)}, u32[]{:S(2)}) %collective-permute-start.8) | collective-permute-done | bytes 196640 | tf_op jit(solution)/shard_map/ppermute | solution.py:608
  81.0 1.8 %collective-permute-start.12 = (bf16[800,512]{1,0:T(8,128)(2,1)S(1)}, bf16[800,512]{1,0:T(8,128)(2,1)S(1)}, u32[]{:S(2)}, u32[]{:S(2)}) collective-permute-start(bf16[800,512]{1,0:T(8,128)(2,1)S(1)} %get-tuple-element.189), channel_id=1, source_target_pairs={{0,4},{1,3},{2,6},{3,1},{4,0},{5,7},{6,2},{7,5},{8,12},{9,11},{10,... | collective-permute-start | bytes 2457608 | tf_op jit(solution)/shard_map/ppermute | solution.py:608
  82.8 2.6 %collective-permute-start.9 = (bf16[192,512]{1,0:T(8,128)(2,1)S(1)}, bf16[192,512]{1,0:T(8,128)(2,1)S(1)}, u32[]{:S(2)}, u32[]{:S(2)}) collective-permute-start(bf16[192,512]{1,0:T(8,128)(2,1)S(1)} %get-tuple-element.181.refs_0_), channel_id=1, source_target_pairs={{0,16},{1,17},{2,18},{3,19},{4,20},{5,21},{6,22},{7,23},{8,24},{9,... | collective-permute-start | bytes 589832 | tf_op jit(solution)/shard_map/ppermute | solution.py:608
  85.3 8.7 %collective-permute-done.9.refs_1_ = bf16[192,512]{1,0:T(8,128)(2,1)S(1)} collective-permute-done((bf16[192,512]{1,0:T(8,128)(2,1)S(1)}, bf16[192,512]{1,0:T(8,128)(2,1)S(1)}, u32[]{:S(2)}, u32[]{:S(2)}) %collective-permute-start.9) | collective-permute-done | bytes 196640 | tf_op jit(solution)/shard_map/ppermute | solution.py:608
  95.3 1.6 %collective-permute-start.11 = (bf16[192,512]{1,0:T(8,128)(2,1)S(1)}, bf16[192,512]{1,0:T(8,128)(2,1)S(1)}, u32[]{:S(2)}, u32[]{:S(2)}) collective-permute-start(bf16[192,512]{1,0:T(8,128)(2,1)S(1)} %get-tuple-element.187.refs_0_), channel_id=1, source_target_pairs={{0,8},{1,9},{2,10},{3,11},{4,12},{5,13},{6,14},{7,15},{8,0},{9,1},... | collective-permute-start | bytes 589832 | tf_op jit(solution)/shard_map/ppermute | solution.py:608
  96.9 5.3 %collective-permute-done.11.refs_1_ = bf16[192,512]{1,0:T(8,128)(2,1)S(1)} collective-permute-done((bf16[192,512]{1,0:T(8,128)(2,1)S(1)}, bf16[192,512]{1,0:T(8,128)(2,1)S(1)}, u32[]{:S(2)}, u32[]{:S(2)}) %collective-permute-start.11) | collective-permute-done | bytes 196640 | tf_op jit(solution)/shard_map/ppermute | solution.py:608
  102.7 1.6 %collective-permute-start.15 = (bf16[224,512]{1,0:T(8,128)(2,1)S(1)}, bf16[224,512]{1,0:T(8,128)(2,1)S(1)}, u32[]{:S(2)}, u32[]{:S(2)}) collective-permute-start(bf16[224,512]{1,0:T(8,128)(2,1)S(1)} %get-tuple-element.199), channel_id=1, source_target_pairs={{0,8},{1,9},{2,10},{3,11},{4,12},{5,13},{6,14},{7,15},{8,0},{9,1},... | collective-permute-start | bytes 688136 | tf_op jit(solution)/shard_map/ppermute | solution.py:608
  104.4 4.8 %collective-permute-done.15.refs_1_ = bf16[224,512]{1,0:T(8,128)(2,1)S(1)} collective-permute-done((bf16[224,512]{1,0:T(8,128)(2,1)S(1)}, bf16[224,512]{1,0:T(8,128)(2,1)S(1)}, u32[]{:S(2)}, u32[]{:S(2)}) %collective-permute-start.15) | collective-permute-done | bytes 229408 | tf_op jit(solution)/shard_map/ppermute | solution.py:608
  111.1 2.8 %collective-permute-start.17 = (bf16[224,512]{1,0:T(8,128)(2,1)S(1)}, bf16[224,512]{1,0:T(8,128)(2,1)S(1)}, u32[]{:S(2)}, u32[]{:S(2)}) collective-permute-start(bf16[224,512]{1,0:T(8,128)(2,1)S(1)} %get-tuple-element.205), channel_id=1, source_target_pairs={{0,16},{1,17},{2,18},{3,19},{4,20},{5,21},{6,22},{7,23},{8,24},{9,... | collective-permute-start | bytes 688136 | tf_op jit(solution)/shard_map/ppermute | solution.py:608
  113.9 8.0 %collective-permute-done.17.refs_1_ = bf16[224,512]{1,0:T(8,128)(2,1)S(1)} collective-permute-done((bf16[224,512]{1,0:T(8,128)(2,1)S(1)}, bf16[224,512]{1,0:T(8,128)(2,1)S(1)}, u32[]{:S(2)}, u32[]{:S(2)}) %collective-permute-start.17) | collective-permute-done | bytes 229408 | tf_op jit(solution)/shard_map/ppermute | solution.py:608
  123.9 5.8 %collective-permute-done.19.refs_1_ = bf16[192,512]{1,0:T(8,128)(2,1)S(1)} collective-permute-done((bf16[192,512]{1,0:T(8,128)(2,1)S(1)}, bf16[192,512]{1,0:T(8,128)(2,1)S(1)}, u32[]{:S(2)}, u32[]{:S(2)}) %collective-permute-start.19) | collective-permute-done | bytes 196640 | tf_op jit(solution)/shard_map/ppermute | solution.py:608
  129.7 1.7 %collective-permute-start.20 = (bf16[384,512]{1,0:T(8,128)(2,1)S(1)}, bf16[384,512]{1,0:T(8,128)(2,1)S(1)}, u32[]{:S(2)}, u32[]{:S(2)}) collective-permute-start(bf16[384,512]{1,0:T(8,128)(2,1)S(1)} %get-tuple-element.216.refs_0_), channel_id=1, source_target_pairs={{0,2},{1,5},{2,0},{3,7},{4,6},{5,1},{6,4},{7,3},{8,10},{9,13},{10,... | collective-permute-start | bytes 1179656 | tf_op jit(solution)/shard_map/ppermute | solution.py:608
  131.4 2.8 %feed_result.1 = (f32[2048,512]{1,0:T(8,128)}, f32[512,2048]{1,0:T(8,128)}, f32[8,128]{1,0:T(8,128)S(1)}) custom-call(bf16[1536,512]{1,0:T(8,128)(2,1)S(1)} %get-tuple-element.209.refs_0_, bf16[1536,512]{1,0:T(8,128)(2,1)S(1)} %collective-permute-done.18.refs_1_, f32[8,128]{1,0:T(8,128)S(1)} %get-tuple-element.212.refs_2_), custom_call_target="tpu_custom_call" | custom-call | flops 12000000000 | bytes 1048576 | tf_op jit(solution)/shard_map/feed_result/pallas_call | solution.py:59
  135.6 1.9 %collective-permute-done.20.refs_1_ = bf16[384,512]{1,0:T(8,128)(2,1)S(1)} collective-permute-done((bf16[384,512]{1,0:T(8,128)(2,1)S(1)}, bf16[384,512]{1,0:T(8,128)(2,1)S(1)}, u32[]{:S(2)}, u32[]{:S(2)}) %collective-permute-start.20) | collective-permute-done | bytes 393248 | tf_op jit(solution)/shard_map/ppermute | solution.py:608
  137.6 1.6 collective-permute-start.21
  139.1 10.5 %collective-permute-done.21.refs_1_ = bf16[768,512]{1,0:T(8,128)(2,1)S(1)} collective-permute-done((bf16[768,512]{1,0:T(8,128)(2,1)S(1)}, bf16[768,512]{1,0:T(8,128)(2,1)S(1)}, u32[]{:S(2)}, u32[]{:S(2)}) %collective-permute-start.21) | collective-permute-done | bytes 786464 | tf_op jit(solution)/shard_map/ppermute | solution.py:608
  149.8 1.8 %own_result.1 = (f32[2048,512]{1,0:T(8,128)}, f32[512,2048]{1,0:T(8,128)}, f32[512,512]{1,0:T(8,128)}, f32[512,512]{1,0:T(8,128)}, f32[512,512]{1,0:T(8,128)}, /*index=5*/f32[512,512]{1,0:T(8,128)}, f32[8,128]{1,0:T(8,128)S(1)}) custom-call(bf16[1568,512]{1,0:T(8,128)(2,1)S(1)} %get-tuple-element.221.refs_0_.refs_7_, ...), custom_call_target="tpu_custom_call", output_to_operand_aliasing={{0}: (1, {}), {1}: (2, {})} | custom-call | flops 6000000000 | bytes 1048576 | tf_op jit(solution)/shard_map/own_result/pallas_call | solution.py:59
  151.6 1.7 %collective-permute-done.22.refs_0_ = bf16[1568,512]{1,0:T(8,128)(2,1)S(1)} collective-permute-done((bf16[1568,512]{1,0:T(8,128)(2,1)S(1)}, bf16[1568,512]{1,0:T(8,128)(2,1)S(1)}, u32[]{:S(2)}, u32[]{:S(2)}) %collective-permute-start.22) | collective-permute-done | bytes 1605664 | tf_op jit(solution)/shard_map/ppermute | solution.py:608
  153.3 2.4 %other_result.1 = (f32[2048,512]{1,0:T(8,128)}, f32[512,2048]{1,0:T(8,128)}, f32[512,512]{1,0:T(8,128)}, f32[512,512]{1,0:T(8,128)}, f32[512,512]{1,0:T(8,128)},...) custom-call(bf16[1568,512]{1,0:T(8,128)(2,1)S(1)} %collective-permut, ...), custom_call_target="tpu_custom_call", output_to_operand_aliasing={{0}: (1, {}), {1}: (2, {}), {2}: (3, {}), {3}: (4, {}), {4}... | custom-call | flops 6000000000 | bytes 1048576 | tf_op jit(solution)/shard_map/other_result/pallas_call | solution.py:59
  (52 shorter events, 10.0 us)
Async XLA Ops:
  2.3 3.3 %collective-permute-start.1 = (bf16[2,256,512]{2,1,0:T(8,128)(2,1)S(1)}, bf16[2,256,512]{2,1,0:T(8,128)(2,1)S(1)}, u32[]{:S(2)}, u32[]{:S(2)}) collective-permute-start(bf16[2,256,512]{2,1,0:T(8,128)(2,1)S(1)} %get-tuple-element.129), channel_id=1, source_target_pairs={{0,1},{1,0},{2,3},{3,2},{4,5},{5,4},{6,7},{7,6},{8,9},{9,8},{10,11... | collective-permute-start | bytes 1572872 | tf_op jit(solution)/shard_map/ppermute | solution.py:677
  2.8 2.6 %copy-start.3 = (f32[32,8]{0,1:T(8,128)S(1)}, f32[32,8]{0,1:T(8,128)}, u32[]{:S(2)}) copy-start(f32[32,8]{0,1:T(8,128)} %param.27) | copy-start | bytes 3076
  2.8 2.8 %copy-start = (f32[512]{0:T(512)S(1)}, f32[512]{0:T(512)}, u32[]{:S(2)}) copy-start(f32[512]{0:T(512)} %param.24) | copy-start | bytes 6148
  2.8 2.8 %copy-start.1 = (f32[512]{0:T(512)S(1)}, f32[512]{0:T(512)}, u32[]{:S(2)}) copy-start(f32[512]{0:T(512)} %param.19) | copy-start | bytes 6148
  2.8 2.8 %copy-start.2 = (s32[2,1]{0,1:T(1,128)S(1)}, s32[2,1]{0,1:T(1,128)}, u32[]{:S(2)}) copy-start(s32[2,1]{0,1:T(1,128)} %param.18) | copy-start | bytes 28
  2.8 2.8 %collective-permute-start.2 = (s32[2,2,256]{2,1,0:T(2,128)S(1)}, s32[2,2,256]{2,1,0:T(2,128)S(1)}, u32[]{:S(2)}, u32[]{:S(2)}) collective-permute-start(s32[2,2,256]{2,1,0:T(2,128)S(1)} %get-tuple-element.131), channel_id=1, source_target_pairs={{0,1},{1,0},{2,3},{3,2},{4,5},{5,4},{6,7},{7,6},{8,9},{9,8},{10,11... | collective-permute-start | bytes 12296 | tf_op jit(solution)/shard_map/ppermute | solution.py:677
  5.0 17.2 %collective-permute-start = (bf16[2,256,512]{2,1,0:T(8,128)(2,1)S(1)}, bf16[2,256,512]{2,1,0:T(8,128)(2,1)S(1)}, u32[]{:S(2)}, u32[]{:S(2)}) collective-permute-start(bf16[2,256,512]{2,1,0:T(8,128)(2,1)S(1)} %get-tuple-element.127), channel_id=1, source_target_pairs={{0,1},{1,0},{2,3},{3,2},{4,5},{5,4},{6,7},{7,6},{8,9},{9,8},{10,11... | collective-permute-start | bytes 1572872 | tf_op jit(solution)/shard_map/ppermute | solution.py:677
  38.7 8.5 %collective-permute-start.4 = (bf16[1536,512]{1,0:T(8,128)(2,1)S(1)}, bf16[1536,512]{1,0:T(8,128)(2,1)S(1)}, u32[]{:S(2)}, u32[]{:S(2)}) collective-permute-start(bf16[1536,512]{1,0:T(8,128)(2,1)S(1)} %get-tuple-element.151), channel_id=1, source_target_pairs={{0,1},{1,0},{2,3},{3,2},{4,5},{5,4},{6,7},{7,6},{8,9},{9,8},{10,11... | collective-permute-start | bytes 4718600 | tf_op jit(solution)/shard_map/ppermute | solution.py:608
  47.6 13.0 %collective-permute-start.5 = (bf16[768,512]{1,0:T(8,128)(2,1)S(1)}, bf16[768,512]{1,0:T(8,128)(2,1)S(1)}, u32[]{:S(2)}, u32[]{:S(2)}) collective-permute-start(bf16[768,512]{1,0:T(8,128)(2,1)S(1)} %get-tuple-element.156), channel_id=1, source_target_pairs={{0,2},{1,5},{2,0},{3,7},{4,6},{5,1},{6,4},{7,3},{8,10},{9,13},{10,... | collective-permute-start | bytes 2359304 | tf_op jit(solution)/shard_map/ppermute | solution.py:608
  60.8 8.1 %collective-permute-start.6 = (bf16[384,512]{1,0:T(8,128)(2,1)S(1)}, bf16[384,512]{1,0:T(8,128)(2,1)S(1)}, u32[]{:S(2)}, u32[]{:S(2)}) collective-permute-start(bf16[384,512]{1,0:T(8,128)(2,1)S(1)} %get-tuple-element.172), channel_id=1, source_target_pairs={{0,4},{1,3},{2,6},{3,1},{4,0},{5,7},{6,2},{7,5},{8,12},{9,11},{10,... | collective-permute-start | bytes 1179656 | tf_op jit(solution)/shard_map/ppermute | solution.py:608
  73.1 7.5 %collective-permute-start.10 = (bf16[1568,512]{1,0:T(8,128)(2,1)S(1)}, bf16[1568,512]{1,0:T(8,128)(2,1)S(1)}, u32[]{:S(2)}, u32[]{:S(2)}) collective-permute-start(bf16[1568,512]{1,0:T(8,128)(2,1)S(1)} %get-tuple-element.183), channel_id=1, source_target_pairs={{0,1},{1,0},{2,3},{3,2},{4,5},{5,4},{6,7},{7,6},{8,9},{9,8},{10,11... | collective-permute-start | bytes 4816904 | tf_op jit(solution)/shard_map/ppermute | solution.py:608
  73.2 7.4 %collective-permute-start.8 = (bf16[192,512]{1,0:T(8,128)(2,1)S(1)}, bf16[192,512]{1,0:T(8,128)(2,1)S(1)}, u32[]{:S(2)}, u32[]{:S(2)}) collective-permute-start(bf16[192,512]{1,0:T(8,128)(2,1)S(1)} %get-tuple-element.179), channel_id=1, source_target_pairs={{0,8},{1,9},{2,10},{3,11},{4,12},{5,13},{6,14},{7,15},{8,0},{9,1},... | collective-permute-start | bytes 589832 | tf_op jit(solution)/shard_map/ppermute | solution.py:608
  81.0 13.1 %collective-permute-start.12 = (bf16[800,512]{1,0:T(8,128)(2,1)S(1)}, bf16[800,512]{1,0:T(8,128)(2,1)S(1)}, u32[]{:S(2)}, u32[]{:S(2)}) collective-permute-start(bf16[800,512]{1,0:T(8,128)(2,1)S(1)} %get-tuple-element.189), channel_id=1, source_target_pairs={{0,4},{1,3},{2,6},{3,1},{4,0},{5,7},{6,2},{7,5},{8,12},{9,11},{10,... | collective-permute-start | bytes 2457608 | tf_op jit(solution)/shard_map/ppermute | solution.py:608
  82.8 11.3 %collective-permute-start.9 = (bf16[192,512]{1,0:T(8,128)(2,1)S(1)}, bf16[192,512]{1,0:T(8,128)(2,1)S(1)}, u32[]{:S(2)}, u32[]{:S(2)}) collective-permute-start(bf16[192,512]{1,0:T(8,128)(2,1)S(1)} %get-tuple-element.181.refs_0_), channel_id=1, source_target_pairs={{0,16},{1,17},{2,18},{3,19},{4,20},{5,21},{6,22},{7,23},{8,24},{9,... | collective-permute-start | bytes 589832 | tf_op jit(solution)/shard_map/ppermute | solution.py:608
  94.3 8.3 %collective-permute-start.14 = (bf16[416,512]{1,0:T(8,128)(2,1)S(1)}, bf16[416,512]{1,0:T(8,128)(2,1)S(1)}, u32[]{:S(2)}, u32[]{:S(2)}) collective-permute-start(bf16[416,512]{1,0:T(8,128)(2,1)S(1)} %get-tuple-element.195), channel_id=1, source_target_pairs={{0,2},{1,5},{2,0},{3,7},{4,6},{5,1},{6,4},{7,3},{8,10},{9,13},{10,... | collective-permute-start | bytes 1277960 | tf_op jit(solution)/shard_map/ppermute | solution.py:608
  95.3 6.8 %collective-permute-start.11 = (bf16[192,512]{1,0:T(8,128)(2,1)S(1)}, bf16[192,512]{1,0:T(8,128)(2,1)S(1)}, u32[]{:S(2)}, u32[]{:S(2)}) collective-permute-start(bf16[192,512]{1,0:T(8,128)(2,1)S(1)} %get-tuple-element.187.refs_0_), channel_id=1, source_target_pairs={{0,8},{1,9},{2,10},{3,11},{4,12},{5,13},{6,14},{7,15},{8,0},{9,1},... | collective-permute-start | bytes 589832 | tf_op jit(solution)/shard_map/ppermute | solution.py:608
  102.2 7.8 %collective-permute-start.13 = (bf16[384,512]{1,0:T(8,128)(2,1)S(1)}, bf16[384,512]{1,0:T(8,128)(2,1)S(1)}, u32[]{:S(2)}, u32[]{:S(2)}) collective-permute-start(bf16[384,512]{1,0:T(8,128)(2,1)S(1)} %get-tuple-element.193.refs_0_), channel_id=1, source_target_pairs={{0,4},{1,3},{2,6},{3,1},{4,0},{5,7},{6,2},{7,5},{8,12},{9,11},{10,... | collective-permute-start | bytes 1179656 | tf_op jit(solution)/shard_map/ppermute | solution.py:608
  102.7 6.4 %collective-permute-start.15 = (bf16[224,512]{1,0:T(8,128)(2,1)S(1)}, bf16[224,512]{1,0:T(8,128)(2,1)S(1)}, u32[]{:S(2)}, u32[]{:S(2)}) collective-permute-start(bf16[224,512]{1,0:T(8,128)(2,1)S(1)} %get-tuple-element.199), channel_id=1, source_target_pairs={{0,8},{1,9},{2,10},{3,11},{4,12},{5,13},{6,14},{7,15},{8,0},{9,1},... | collective-permute-start | bytes 688136 | tf_op jit(solution)/shard_map/ppermute | solution.py:608
  110.1 12.1 %collective-permute-start.16 = (bf16[768,512]{1,0:T(8,128)(2,1)S(1)}, bf16[768,512]{1,0:T(8,128)(2,1)S(1)}, u32[]{:S(2)}, u32[]{:S(2)}) collective-permute-start(bf16[768,512]{1,0:T(8,128)(2,1)S(1)} %get-tuple-element.203.refs_0_), channel_id=1, source_target_pairs={{0,2},{1,5},{2,0},{3,7},{4,6},{5,1},{6,4},{7,3},{8,10},{9,13},{10,... | collective-permute-start | bytes 2359304 | tf_op jit(solution)/shard_map/ppermute | solution.py:608
  111.1 10.8 %collective-permute-start.17 = (bf16[224,512]{1,0:T(8,128)(2,1)S(1)}, bf16[224,512]{1,0:T(8,128)(2,1)S(1)}, u32[]{:S(2)}, u32[]{:S(2)}) collective-permute-start(bf16[224,512]{1,0:T(8,128)(2,1)S(1)} %get-tuple-element.205), channel_id=1, source_target_pairs={{0,16},{1,17},{2,18},{3,19},{4,20},{5,21},{6,22},{7,23},{8,24},{9,... | collective-permute-start | bytes 688136 | tf_op jit(solution)/shard_map/ppermute | solution.py:608
  122.3 9.2 %collective-permute-start.18 = (bf16[1536,512]{1,0:T(8,128)(2,1)S(1)}, bf16[1536,512]{1,0:T(8,128)(2,1)S(1)}, u32[]{:S(2)}, u32[]{:S(2)}) collective-permute-start(bf16[1536,512]{1,0:T(8,128)(2,1)S(1)} %get-tuple-element.209.refs_0_), channel_id=1, source_target_pairs={{0,1},{1,0},{2,3},{3,2},{4,5},{5,4},{6,7},{7,6},{8,9},{9,8},{10,11... | collective-permute-start | bytes 4718600 | tf_op jit(solution)/shard_map/ppermute | solution.py:608
  122.3 7.3 %collective-permute-start.19 = (bf16[192,512]{1,0:T(8,128)(2,1)S(1)}, bf16[192,512]{1,0:T(8,128)(2,1)S(1)}, u32[]{:S(2)}, u32[]{:S(2)}) collective-permute-start(bf16[192,512]{1,0:T(8,128)(2,1)S(1)} %get-tuple-element.210.refs_0_), channel_id=1, source_target_pairs={{0,8},{1,9},{2,10},{3,11},{4,12},{5,13},{6,14},{7,15},{8,0},{9,1},... | collective-permute-start | bytes 589832 | tf_op jit(solution)/shard_map/ppermute | solution.py:608
  123.4 10.9 %collective-permute-start.3 = (bf16[2,256,512]{2,1,0:T(8,128)(2,1)S(1)}, bf16[2,256,512]{2,1,0:T(8,128)(2,1)S(1)}, u32[]{:S(2)}, u32[]{:S(2)}) collective-permute-start(bf16[2,256,512]{2,1,0:T(8,128)(2,1)S(1)} %get-tuple-element.141), channel_id=1, source_target_pairs={{0,1},{1,0},{2,3},{3,2},{4,5},{5,4},{6,7},{7,6},{8,9},{9,8},{10,11... | collective-permute-start | bytes 1572872 | tf_op jit(solution)/shard_map/ppermute | solution.py:677
  123.5 10.7 %collective-permute-start.7 = (bf16[2,256,512]{2,1,0:T(8,128)(2,1)S(1)}, bf16[2,256,512]{2,1,0:T(8,128)(2,1)S(1)}, u32[]{:S(2)}, u32[]{:S(2)}) collective-permute-start(bf16[2,256,512]{2,1,0:T(8,128)(2,1)S(1)} %get-tuple-element.177), channel_id=1, source_target_pairs={{0,1},{1,0},{2,3},{3,2},{4,5},{5,4},{6,7},{7,6},{8,9},{9,8},{10,11... | collective-permute-start | bytes 1572872 | tf_op jit(solution)/shard_map/ppermute | solution.py:677
  129.7 7.8 %collective-permute-start.20 = (bf16[384,512]{1,0:T(8,128)(2,1)S(1)}, bf16[384,512]{1,0:T(8,128)(2,1)S(1)}, u32[]{:S(2)}, u32[]{:S(2)}) collective-permute-start(bf16[384,512]{1,0:T(8,128)(2,1)S(1)} %get-tuple-element.216.refs_0_), channel_id=1, source_target_pairs={{0,2},{1,5},{2,0},{3,7},{4,6},{5,1},{6,4},{7,3},{8,10},{9,13},{10,... | collective-permute-start | bytes 1179656 | tf_op jit(solution)/shard_map/ppermute | solution.py:608
  137.6 12.1 %collective-permute-start.21 = (bf16[768,512]{1,0:T(8,128)(2,1)S(1)}, bf16[768,512]{1,0:T(8,128)(2,1)S(1)}, u32[]{:S(2)}, u32[]{:S(2)}) collective-permute-start(bf16[768,512]{1,0:T(8,128)(2,1)S(1)} %get-tuple-element.218.refs_0_), channel_id=1, source_target_pairs={{0,4},{1,3},{2,6},{3,1},{4,0},{5,7},{6,2},{7,5},{8,12},{9,11},{10,... | collective-permute-start | bytes 2359304 | tf_op jit(solution)/shard_map/ppermute | solution.py:608
  149.7 3.5 %collective-permute-start.22 = (bf16[1568,512]{1,0:T(8,128)(2,1)S(1)}, bf16[1568,512]{1,0:T(8,128)(2,1)S(1)}, u32[]{:S(2)}, u32[]{:S(2)}) collective-permute-start(bf16[1568,512]{1,0:T(8,128)(2,1)S(1)} %get-tuple-element.221.refs_0_.refs_7_), channel_id=1, source_target_pairs={{0,1},{1,0},{2,3},{3,2},{4,5},{5,4},{6,7},{7,6},{8,9},{9,8},{10,11... | collective-permute-start | bytes 4816904 | tf_op jit(solution)/shard_map/ppermute | solution.py:608

commit v3 on v2

--- a/solution.py
+++ b/solution.py
@@ -791,6 +791,10 @@
     grad_down = None
     all_rows = sds((rows, slots, half, width), BF)
     c_piece.land()
+    output, grad_input = call(
+        place_kernel, "place", 1, (out_own, out_got, in_own, in_got), [whole()] * 4,
+        (all_rows, all_rows), out_specs=[far(), far()], scratch=[dma((4 * rows,))], who=who[0],
+    )
     a.land()
     c_piece.land()
     a.land()
@@ -809,10 +813,6 @@
                 vmem=VMEM[7],
                 who=who[0],
             )
-            output, grad_input = call(
-                place_kernel, "place", 1, (out_own, out_got, in_own, in_got), [whole()] * 4,
-                (all_rows, all_rows), out_specs=[far(), far()], scratch=[dma((4 * rows,))], who=who[0],
-            )
     own, got = c_piece.done()
     shapes = (sds((ff, width), F32), sds((width, ff), F32), square, square, square, square)
     result_scratch = [vm((6, width // 2, width), F32), dma((6,))]

time: 156 us -> 156 us (level)
  waiting for transfers between devices: 53.3 us -> 50.4 us
  starting transfers between devices: 26.1 us -> 28.5 us
    ppermute x18, waiting for transfers between devices: 53.3 us -> 50.4 us  [fly(): lax.ppermute(self.send, ('dp', 'seq'), swap_pairs(self.dp, self.steps[0][...]
    ppermute x18, starting transfers between devices: 24.4 us -> 26.8 us  [fly(): lax.ppermute(self.send, ('dp', 'seq'), swap_pairs(self.dp, self.steps[0][...]
  transfers between devices with their start and end apart: 23 -> 23, of which waited for: 12 -> 12; matrix products, arithmetic and copies ran while one was open for 0% -> 0% of each run, Pallas kernels for 31% -> 32%
where the time goes in v3:
time: 156 us; the launch traced here: 155 us
  Pallas kernels  75.1 us (48%)
  waiting for transfers between devices  50.4 us (32%)
  starting transfers between devices  28.5 us (18%)
    pallas_call x29, Pallas kernels, call(): pl.pallas_call(body, grid=(grid,), in_specs=list(in_specs) + [whole()] *...  75.1 us
    ppermute x18, waiting for transfers between devices, fly(): lax.ppermute(self.send, ('dp', 'seq'), swap_pairs(self.dp, self.steps[0][...  50.4 us
    ppermute x18, starting transfers between devices, fly(): lax.ppermute(self.send, ('dp', 'seq'), swap_pairs(self.dp, self.steps[0][...  26.8 us
  transfers between devices with their start and end apart: 23, of which 12 were waited for; matrix products, arithmetic and copies ran while one was open for 0% of the time, Pallas kernels for 32%

profile of v3, /device:TPU:0, one launch (start us, length us, event | category | flops | bytes accessed | tf_op | source)
XLA Modules:
  0.0 155.3 jit_solution(2106814546573609791)
XLA Ops:
  0.6 1.7 %pick.1 = (bf16[2,256,512]{2,1,0:T(8,128)(2,1)S(1)}, s32[2,2,256]{2,1,0:T(2,128)S(1)}, s32[2,2,256]{2,1,0:T(2,128)S(1)}, f32[8,128]{1,0:T(8,128)}) custom-call(bf16[2,2,256,512]{3,2,1,0:T(8,128)(2,1)} %refs_0_.3, s32[2,2,256]{2,1,0:T(2,128)} %refs_1_.3, s32[2,2,256]{2,1,0:T(2,128)} %refs_2_.1), custom_call_target="tpu_custom_call" | custom-call | flops 3000000000 | bytes 1048576 | tf_op jit(solution)/shard_map/pick/pallas_call | solution.py:59
  3.0 2.0 %pick_rest.1 = (bf16[2,256,512]{2,1,0:T(8,128)(2,1)S(1)}, bf16[2,256,512]{2,1,0:T(8,128)(2,1)S(1)}, bf16[2,256,512]{2,1,0:T(8,128)(2,1)S(1)}, f32[8,128]{1,0:T(8,128)}) custom-call(bf16[2,2,256,512]{3,2,1,0:T(8,128)(2,1)} %refs_0_.3, bf16[2,2,256,512]{3,2,1,0:T(8,128)(2,1)} %refs_1_.2), custom_call_target="tpu_custom_call" | custom-call | flops 3000000000 | bytes 1048576 | tf_op jit(solution)/shard_map/pick_rest/pallas_call | solution.py:59
  5.7 16.4 %attend_forward.1 = (bf16[2,512,512]{2,1,0:T(8,128)(2,1)S(1)}, bf16[2,512,512]{2,1,0:T(8,128)(2,1)S(1)}, bf16[2,4,512,128]{3,2,1,0:T(8,128)(2,1)S(1)}, bf16[2,4,...) custom-call(s32[2]{0:T(128)S(1)} %bitcast.12, ...), custom_call_target="tpu_custom_call" | custom-call | flops 41999998976 | bytes 1048576 | tf_op jit(solution)/shard_map/attend_forward/pallas_call | solution.py:59
  22.1 16.6 %feed_first.1 = (bf16[2,512,512]{2,1,0:T(8,128)(2,1)S(1)}, bf16[2,512,512]{2,1,0:T(8,128)(2,1)S(1)}, f32[2,512,512]{2,1,0:T(8,128)S(1)}, f32[2,512,512]{2,1,0:T(...) custom-call(bf16[2,256,512]{2,1,0:T(8,128)(2,1)S(1)} %get-tuple-element.126.refs_0_, ...), custom_call_target="tpu_custom_call" | custom-call | flops 44999999488 | bytes 1048576 | tf_op jit(solution)/shard_map/feed_first/pallas_call | solution.py:59
  38.8 8.4 %feed_third.1 = (f32[2,512,512]{2,1,0:T(8,128)S(1)}, f32[2,512,512]{2,1,0:T(8,128)S(1)}, bf16[2,256,512]{2,1,0:T(8,128)(2,1)S(1)}, bf16[2,256,512]{2,1,0:T(8,128...) custom-call(bf16[2,512,512]{2,1,0:T(8,128)(2,1)S(1)} %get-tuple-elem, ...), custom_call_target="tpu_custom_call", output_to_operand_aliasing={{0}: (2, {}), {1}: (3, {})} | custom-call | flops 24000000000 | bytes 1048576 | tf_op jit(solution)/shard_map/feed_third/pallas_call | solution.py:59
  47.6 3.0 %collective-permute-start.5 = (bf16[768,512]{1,0:T(8,128)(2,1)S(1)}, bf16[768,512]{1,0:T(8,128)(2,1)S(1)}, u32[]{:S(2)}, u32[]{:S(2)}) collective-permute-start(bf16[768,512]{1,0:T(8,128)(2,1)S(1)} %get-tuple-element.156), channel_id=1, source_target_pairs={{0,2},{1,5},{2,0},{3,7},{4,6},{5,1},{6,4},{7,3},{8,10},{9,13},{10,... | collective-permute-start | bytes 2359304 | tf_op jit(solution)/shard_map/ppermute | solution.py:608
  50.6 6.0 %attend_backward.2 = (bf16[2,2,512,128]{3,2,1,0:T(8,128)(2,1)S(1)}, bf16[2,2,512,128]{3,2,1,0:T(8,128)(2,1)S(1)}, bf16[2,2,512,128]{3,2,1,0:T(8,128)(2,1)S(1)}, f32[4,1,1024]{2,1,0:T(1,128)S(1)}, f32[8,128]{1,0:T(8,128)S(1)}) custom-call(bf16[2,4,2,512,512]{4,3,2,1,0:T(8,128)(2,1)S(1)} %get-tuple-element.144.refs_0_, ...), custom_call_target="tpu_custom_call" | custom-call | flops 17999998976 | bytes 1048576 | tf_op jit(solution)/shard_map/attend_backward/pallas_call | solution.py:59
  56.6 3.9 %collective-permute-done.5.refs_1_ = bf16[768,512]{1,0:T(8,128)(2,1)S(1)} collective-permute-done((bf16[768,512]{1,0:T(8,128)(2,1)S(1)}, bf16[768,512]{1,0:T(8,128)(2,1)S(1)}, u32[]{:S(2)}, u32[]{:S(2)}) %collective-permute-start.5) | collective-permute-done | bytes 786464 | tf_op jit(solution)/shard_map/ppermute | solution.py:608
  60.8 2.1 %collective-permute-start.6 = (bf16[384,512]{1,0:T(8,128)(2,1)S(1)}, bf16[384,512]{1,0:T(8,128)(2,1)S(1)}, u32[]{:S(2)}, u32[]{:S(2)}) collective-permute-start(bf16[384,512]{1,0:T(8,128)(2,1)S(1)} %get-tuple-element.172), channel_id=1, source_target_pairs={{0,4},{1,3},{2,6},{3,1},{4,0},{5,7},{6,2},{7,5},{8,12},{9,11},{10,... | collective-permute-start | bytes 1179656 | tf_op jit(solution)/shard_map/ppermute | solution.py:608
  62.9 6.0 %attend_backward.3 = (bf16[2,2,512,128]{3,2,1,0:T(8,128)(2,1)S(1)}, bf16[2,2,512,128]{3,2,1,0:T(8,128)(2,1)S(1)}, bf16[2,2,512,128]{3,2,1,0:T(8,128)(2,1)S(1)}, f32[4,1,1024]{2,1,0:T(1,128)S(1)}, f32[8,128]{1,0:T(8,128)S(1)}) custom-call(bf16[2,4,2,512,512]{4,3,2,1,0:T(8,128)(2,1)S(1)} %get-tuple-element.144.refs_0_, ...), custom_call_target="tpu_custom_call" | custom-call | flops 17999998976 | bytes 1048576 | tf_op jit(solution)/shard_map/attend_backward/pallas_call | solution.py:59
  69.0 4.1 %weight_grads.1 = (bf16[1536,512]{1,0:T(8,128)(2,1)S(1)}, bf16[1568,512]{1,0:T(8,128)(2,1)S(1)}, bf16[32,512]{1,0:T(8,128)(2,1)S(1)}, f32[8,128]{1,0:T(8,128)S(1)}) custom-call(bf16[2,512,512]{2,1,0:T(8,128)(2,1)S(1)} %get-tuple-element.164.refs_0_, bf16[2,2,512,128]{3,2,1,0:T(8,128)(2,1)S(1)} %get-tuple-element.154.refs_1_.refs_2_, ...), custom_call_target="tpu_custom_call" | custom-call | flops 8999999488 | bytes 1048576 | tf_op jit(solution)/shard_map/weight_grads/pallas_call | solution.py:59
  73.7 1.8 %collective-permute-start.9 = (bf16[192,512]{1,0:T(8,128)(2,1)S(1)}, bf16[192,512]{1,0:T(8,128)(2,1)S(1)}, u32[]{:S(2)}, u32[]{:S(2)}) collective-permute-start(bf16[192,512]{1,0:T(8,128)(2,1)S(1)} %get-tuple-element.182), channel_id=1, source_target_pairs={{0,8},{1,9},{2,10},{3,11},{4,12},{5,13},{6,14},{7,15},{8,0},{9,1},... | collective-permute-start | bytes 589832 | tf_op jit(solution)/shard_map/ppermute | solution.py:608
  75.4 3.7 %input_grad.1 = (bf16[2,256,512]{2,1,0:T(8,128)(2,1)S(1)}, bf16[2,256,512]{2,1,0:T(8,128)(2,1)S(1)}, f32[8,128]{1,0:T(8,128)S(1)}) custom-call(bf16[2,512,512]{2,1,0:T(8,128)(2,1)S(1)} %get-tuple-element.142.refs_0_, f32[2,512,512]{2,1,0:T(8,128)S(1)} %get-tuple-element.143.refs_1_, bf16[2,2,512,128]{3,2,1,0:T(8,128)(2,1)S(1)} %get-tuple-element.154.refs_1_.refs_2_, ...), custom_call_target="tpu_custom_call" | custom-call | flops 12000000000 | bytes 1048576 | tf_op jit(solution)/shard_map/input_grad/pallas_call | solution.py:59
  81.1 1.7 %collective-permute-start.10 = (bf16[800,512]{1,0:T(8,128)(2,1)S(1)}, bf16[800,512]{1,0:T(8,128)(2,1)S(1)}, u32[]{:S(2)}, u32[]{:S(2)}) collective-permute-start(bf16[800,512]{1,0:T(8,128)(2,1)S(1)} %get-tuple-element.189), channel_id=1, source_target_pairs={{0,4},{1,3},{2,6},{3,1},{4,0},{5,7},{6,2},{7,5},{8,12},{9,11},{10,... | collective-permute-start | bytes 2457608 | tf_op jit(solution)/shard_map/ppermute | solution.py:608
  82.8 2.6 %collective-permute-start.11 = (bf16[192,512]{1,0:T(8,128)(2,1)S(1)}, bf16[192,512]{1,0:T(8,128)(2,1)S(1)}, u32[]{:S(2)}, u32[]{:S(2)}) collective-permute-start(bf16[192,512]{1,0:T(8,128)(2,1)S(1)} %get-tuple-element.191.refs_0_), channel_id=1, source_target_pairs={{0,16},{1,17},{2,18},{3,19},{4,20},{5,21},{6,22},{7,23},{8,24},{9,... | collective-permute-start | bytes 589832 | tf_op jit(solution)/shard_map/ppermute | solution.py:608
  86.8 6.9 %collective-permute-done.11.refs_1_ = bf16[192,512]{1,0:T(8,128)(2,1)S(1)} collective-permute-done((bf16[192,512]{1,0:T(8,128)(2,1)S(1)}, bf16[192,512]{1,0:T(8,128)(2,1)S(1)}, u32[]{:S(2)}, u32[]{:S(2)}) %collective-permute-start.11) | collective-permute-done | bytes 196640 | tf_op jit(solution)/shard_map/ppermute | solution.py:608
  95.4 1.6 %collective-permute-start.13 = (bf16[192,512]{1,0:T(8,128)(2,1)S(1)}, bf16[192,512]{1,0:T(8,128)(2,1)S(1)}, u32[]{:S(2)}, u32[]{:S(2)}) collective-permute-start(bf16[192,512]{1,0:T(8,128)(2,1)S(1)} %get-tuple-element.197.refs_0_), channel_id=1, source_target_pairs={{0,8},{1,9},{2,10},{3,11},{4,12},{5,13},{6,14},{7,15},{8,0},{9,1},... | collective-permute-start | bytes 589832 | tf_op jit(solution)/shard_map/ppermute | solution.py:608
  97.0 4.3 %collective-permute-done.13.refs_1_ = bf16[192,512]{1,0:T(8,128)(2,1)S(1)} collective-permute-done((bf16[192,512]{1,0:T(8,128)(2,1)S(1)}, bf16[192,512]{1,0:T(8,128)(2,1)S(1)}, u32[]{:S(2)}, u32[]{:S(2)}) %collective-permute-start.13) | collective-permute-done | bytes 196640 | tf_op jit(solution)/shard_map/ppermute | solution.py:608
  102.8 1.6 %collective-permute-start.14 = (bf16[224,512]{1,0:T(8,128)(2,1)S(1)}, bf16[224,512]{1,0:T(8,128)(2,1)S(1)}, u32[]{:S(2)}, u32[]{:S(2)}) collective-permute-start(bf16[224,512]{1,0:T(8,128)(2,1)S(1)} %get-tuple-element.201), channel_id=1, source_target_pairs={{0,8},{1,9},{2,10},{3,11},{4,12},{5,13},{6,14},{7,15},{8,0},{9,1},... | collective-permute-start | bytes 688136 | tf_op jit(solution)/shard_map/ppermute | solution.py:608
  104.4 4.4 %collective-permute-done.14.refs_1_ = bf16[224,512]{1,0:T(8,128)(2,1)S(1)} collective-permute-done((bf16[224,512]{1,0:T(8,128)(2,1)S(1)}, bf16[224,512]{1,0:T(8,128)(2,1)S(1)}, u32[]{:S(2)}, u32[]{:S(2)}) %collective-permute-start.14) | collective-permute-done | bytes 229408 | tf_op jit(solution)/shard_map/ppermute | solution.py:608
  109.2 1.5 collective-permute-start.18
  110.8 2.2 %collective-permute-start.15 = (bf16[224,512]{1,0:T(8,128)(2,1)S(1)}, bf16[224,512]{1,0:T(8,128)(2,1)S(1)}, u32[]{:S(2)}, u32[]{:S(2)}) collective-permute-start(bf16[224,512]{1,0:T(8,128)(2,1)S(1)} %get-tuple-element.205), channel_id=1, source_target_pairs={{0,16},{1,17},{2,18},{3,19},{4,20},{5,21},{6,22},{7,23},{8,24},{9,... | collective-permute-start | bytes 688136 | tf_op jit(solution)/shard_map/ppermute | solution.py:608
  113.0 8.2 %collective-permute-done.15.refs_1_ = bf16[224,512]{1,0:T(8,128)(2,1)S(1)} collective-permute-done((bf16[224,512]{1,0:T(8,128)(2,1)S(1)}, bf16[224,512]{1,0:T(8,128)(2,1)S(1)}, u32[]{:S(2)}, u32[]{:S(2)}) %collective-permute-start.15) | collective-permute-done | bytes 229408 | tf_op jit(solution)/shard_map/ppermute | solution.py:608
  123.0 5.8 %collective-permute-done.17.refs_1_ = bf16[192,512]{1,0:T(8,128)(2,1)S(1)} collective-permute-done((bf16[192,512]{1,0:T(8,128)(2,1)S(1)}, bf16[192,512]{1,0:T(8,128)(2,1)S(1)}, u32[]{:S(2)}, u32[]{:S(2)}) %collective-permute-start.17) | collective-permute-done | bytes 196640 | tf_op jit(solution)/shard_map/ppermute | solution.py:608
  128.8 1.5 collective-permute-start.19
  130.4 2.8 %feed_result.1 = (f32[2048,512]{1,0:T(8,128)}, f32[512,2048]{1,0:T(8,128)}, f32[8,128]{1,0:T(8,128)S(1)}) custom-call(bf16[1536,512]{1,0:T(8,128)(2,1)S(1)} %get-tuple-element.215.refs_0_, bf16[1536,512]{1,0:T(8,128)(2,1)S(1)} %collective-permute-done.20.refs_1_, f32[8,128]{1,0:T(8,128)S(1)} %get-tuple-element.216.refs_2_), custom_call_target="tpu_custom_call" | custom-call | flops 12000000000 | bytes 1048576 | tf_op jit(solution)/shard_map/feed_result/pallas_call | solution.py:59
  133.2 3.5 %collective-permute-done.19.refs_1_ = bf16[384,512]{1,0:T(8,128)(2,1)S(1)} collective-permute-done((bf16[384,512]{1,0:T(8,128)(2,1)S(1)}, bf16[384,512]{1,0:T(8,128)(2,1)S(1)}, u32[]{:S(2)}, u32[]{:S(2)}) %collective-permute-start.19) | collective-permute-done | bytes 393248 | tf_op jit(solution)/shard_map/ppermute | solution.py:608
  136.7 2.4 %collective-permute-start.21 = (bf16[768,512]{1,0:T(8,128)(2,1)S(1)}, bf16[768,512]{1,0:T(8,128)(2,1)S(1)}, u32[]{:S(2)}, u32[]{:S(2)}) collective-permute-start(bf16[768,512]{1,0:T(8,128)(2,1)S(1)} %get-tuple-element.218.refs_0_), channel_id=1, source_target_pairs={{0,4},{1,3},{2,6},{3,1},{4,0},{5,7},{6,2},{7,5},{8,12},{9,11},{10,... | collective-permute-start | bytes 2359304 | tf_op jit(solution)/shard_map/ppermute | solution.py:608
  139.1 10.0 %collective-permute-done.21.refs_1_ = bf16[768,512]{1,0:T(8,128)(2,1)S(1)} collective-permute-done((bf16[768,512]{1,0:T(8,128)(2,1)S(1)}, bf16[768,512]{1,0:T(8,128)(2,1)S(1)}, u32[]{:S(2)}, u32[]{:S(2)}) %collective-permute-start.21) | collective-permute-done | bytes 786464 | tf_op jit(solution)/shard_map/ppermute | solution.py:608
  149.3 1.8 %own_result.1 = (f32[2048,512]{1,0:T(8,128)}, f32[512,2048]{1,0:T(8,128)}, f32[512,512]{1,0:T(8,128)}, f32[512,512]{1,0:T(8,128)}, f32[512,512]{1,0:T(8,128)}, /*index=5*/f32[512,512]{1,0:T(8,128)}, f32[8,128]{1,0:T(8,128)S(1)}) custom-call(bf16[1568,512]{1,0:T(8,128)(2,1)S(1)} %get-tuple-element.221.refs_0_.refs_7_, ...), custom_call_target="tpu_custom_call", output_to_operand_aliasing={{0}: (1, {}), {1}: (2, {})} | custom-call | flops 6000000000 | bytes 1048576 | tf_op jit(solution)/shard_map/own_result/pallas_call | solution.py:59
  151.1 1.7 %collective-permute-done.22.refs_0_ = bf16[1568,512]{1,0:T(8,128)(2,1)S(1)} collective-permute-done((bf16[1568,512]{1,0:T(8,128)(2,1)S(1)}, bf16[1568,512]{1,0:T(8,128)(2,1)S(1)}, u32[]{:S(2)}, u32[]{:S(2)}) %collective-permute-start.22) | collective-permute-done | bytes 1605664 | tf_op jit(solution)/shard_map/ppermute | solution.py:608
  152.7 2.4 %other_result.1 = (f32[2048,512]{1,0:T(8,128)}, f32[512,2048]{1,0:T(8,128)}, f32[512,512]{1,0:T(8,128)}, f32[512,512]{1,0:T(8,128)}, f32[512,512]{1,0:T(8,128)},...) custom-call(bf16[1568,512]{1,0:T(8,128)(2,1)S(1)} %collective-permut, ...), custom_call_target="tpu_custom_call", output_to_operand_aliasing={{0}: (1, {}), {1}: (2, {}), {2}: (3, {}), {3}: (4, {}), {4}... | custom-call | flops 6000000000 | bytes 1048576 | tf_op jit(solution)/shard_map/other_result/pallas_call | solution.py:59
  (52 shorter events, 11.5 us)
Async XLA Ops:
  2.3 3.3 %collective-permute-start.1 = (bf16[2,256,512]{2,1,0:T(8,128)(2,1)S(1)}, bf16[2,256,512]{2,1,0:T(8,128)(2,1)S(1)}, u32[]{:S(2)}, u32[]{:S(2)}) collective-permute-start(bf16[2,256,512]{2,1,0:T(8,128)(2,1)S(1)} %get-tuple-element.129), channel_id=1, source_target_pairs={{0,1},{1,0},{2,3},{3,2},{4,5},{5,4},{6,7},{7,6},{8,9},{9,8},{10,11... | collective-permute-start | bytes 1572872 | tf_op jit(solution)/shard_map/ppermute | solution.py:677
  2.8 2.6 %copy-start.3 = (f32[32,8]{0,1:T(8,128)S(1)}, f32[32,8]{0,1:T(8,128)}, u32[]{:S(2)}) copy-start(f32[32,8]{0,1:T(8,128)} %param.27) | copy-start | bytes 3076
  2.8 2.8 %copy-start = (f32[512]{0:T(512)S(1)}, f32[512]{0:T(512)}, u32[]{:S(2)}) copy-start(f32[512]{0:T(512)} %param.24) | copy-start | bytes 6148
  2.8 2.8 %copy-start.1 = (f32[512]{0:T(512)S(1)}, f32[512]{0:T(512)}, u32[]{:S(2)}) copy-start(f32[512]{0:T(512)} %param.19) | copy-start | bytes 6148
  2.8 2.8 %copy-start.2 = (s32[2,1]{0,1:T(1,128)S(1)}, s32[2,1]{0,1:T(1,128)}, u32[]{:S(2)}) copy-start(s32[2,1]{0,1:T(1,128)} %param.18) | copy-start | bytes 28
  2.8 2.8 %collective-permute-start.2 = (s32[2,2,256]{2,1,0:T(2,128)S(1)}, s32[2,2,256]{2,1,0:T(2,128)S(1)}, u32[]{:S(2)}, u32[]{:S(2)}) collective-permute-start(s32[2,2,256]{2,1,0:T(2,128)S(1)} %get-tuple-element.131), channel_id=1, source_target_pairs={{0,1},{1,0},{2,3},{3,2},{4,5},{5,4},{6,7},{7,6},{8,9},{9,8},{10,11... | collective-permute-start | bytes 12296 | tf_op jit(solution)/shard_map/ppermute | solution.py:677
  5.0 17.2 %collective-permute-start = (bf16[2,256,512]{2,1,0:T(8,128)(2,1)S(1)}, bf16[2,256,512]{2,1,0:T(8,128)(2,1)S(1)}, u32[]{:S(2)}, u32[]{:S(2)}) collective-permute-start(bf16[2,256,512]{2,1,0:T(8,128)(2,1)S(1)} %get-tuple-element.127), channel_id=1, source_target_pairs={{0,1},{1,0},{2,3},{3,2},{4,5},{5,4},{6,7},{7,6},{8,9},{9,8},{10,11... | collective-permute-start | bytes 1572872 | tf_op jit(solution)/shard_map/ppermute | solution.py:677
  38.7 8.5 %collective-permute-start.4 = (bf16[1536,512]{1,0:T(8,128)(2,1)S(1)}, bf16[1536,512]{1,0:T(8,128)(2,1)S(1)}, u32[]{:S(2)}, u32[]{:S(2)}) collective-permute-start(bf16[1536,512]{1,0:T(8,128)(2,1)S(1)} %get-tuple-element.151), channel_id=1, source_target_pairs={{0,1},{1,0},{2,3},{3,2},{4,5},{5,4},{6,7},{7,6},{8,9},{9,8},{10,11... | collective-permute-start | bytes 4718600 | tf_op jit(solution)/shard_map/ppermute | solution.py:608
  47.6 13.0 %collective-permute-start.5 = (bf16[768,512]{1,0:T(8,128)(2,1)S(1)}, bf16[768,512]{1,0:T(8,128)(2,1)S(1)}, u32[]{:S(2)}, u32[]{:S(2)}) collective-permute-start(bf16[768,512]{1,0:T(8,128)(2,1)S(1)} %get-tuple-element.156), channel_id=1, source_target_pairs={{0,2},{1,5},{2,0},{3,7},{4,6},{5,1},{6,4},{7,3},{8,10},{9,13},{10,... | collective-permute-start | bytes 2359304 | tf_op jit(solution)/shard_map/ppermute | solution.py:608
  60.8 8.1 %collective-permute-start.6 = (bf16[384,512]{1,0:T(8,128)(2,1)S(1)}, bf16[384,512]{1,0:T(8,128)(2,1)S(1)}, u32[]{:S(2)}, u32[]{:S(2)}) collective-permute-start(bf16[384,512]{1,0:T(8,128)(2,1)S(1)} %get-tuple-element.172), channel_id=1, source_target_pairs={{0,4},{1,3},{2,6},{3,1},{4,0},{5,7},{6,2},{7,5},{8,12},{9,11},{10,... | collective-permute-start | bytes 1179656 | tf_op jit(solution)/shard_map/ppermute | solution.py:608
  73.1 7.6 %collective-permute-start.8 = (bf16[1568,512]{1,0:T(8,128)(2,1)S(1)}, bf16[1568,512]{1,0:T(8,128)(2,1)S(1)}, u32[]{:S(2)}, u32[]{:S(2)}) collective-permute-start(bf16[1568,512]{1,0:T(8,128)(2,1)S(1)} %get-tuple-element.179), channel_id=1, source_target_pairs={{0,1},{1,0},{2,3},{3,2},{4,5},{5,4},{6,7},{7,6},{8,9},{9,8},{10,11... | collective-permute-start | bytes 4816904 | tf_op jit(solution)/shard_map/ppermute | solution.py:608
  73.2 12.3 %collective-permute-start.3 = (bf16[2,256,512]{2,1,0:T(8,128)(2,1)S(1)}, bf16[2,256,512]{2,1,0:T(8,128)(2,1)S(1)}, u32[]{:S(2)}, u32[]{:S(2)}) collective-permute-start(bf16[2,256,512]{2,1,0:T(8,128)(2,1)S(1)} %get-tuple-element.141), channel_id=1, source_target_pairs={{0,1},{1,0},{2,3},{3,2},{4,5},{5,4},{6,7},{7,6},{8,9},{9,8},{10,11... | collective-permute-start | bytes 1572872 | tf_op jit(solution)/shard_map/ppermute | solution.py:677
  73.7 6.9 %collective-permute-start.9 = (bf16[192,512]{1,0:T(8,128)(2,1)S(1)}, bf16[192,512]{1,0:T(8,128)(2,1)S(1)}, u32[]{:S(2)}, u32[]{:S(2)}) collective-permute-start(bf16[192,512]{1,0:T(8,128)(2,1)S(1)} %get-tuple-element.182), channel_id=1, source_target_pairs={{0,8},{1,9},{2,10},{3,11},{4,12},{5,13},{6,14},{7,15},{8,0},{9,1},... | collective-permute-start | bytes 589832 | tf_op jit(solution)/shard_map/ppermute | solution.py:608
  79.2 6.2 %collective-permute-start.7 = (bf16[2,256,512]{2,1,0:T(8,128)(2,1)S(1)}, bf16[2,256,512]{2,1,0:T(8,128)(2,1)S(1)}, u32[]{:S(2)}, u32[]{:S(2)}) collective-permute-start(bf16[2,256,512]{2,1,0:T(8,128)(2,1)S(1)} %get-tuple-element.177), channel_id=1, source_target_pairs={{0,1},{1,0},{2,3},{3,2},{4,5},{5,4},{6,7},{7,6},{8,9},{9,8},{10,11... | collective-permute-start | bytes 1572872 | tf_op jit(solution)/shard_map/ppermute | solution.py:677
  81.1 12.7 %collective-permute-start.10 = (bf16[800,512]{1,0:T(8,128)(2,1)S(1)}, bf16[800,512]{1,0:T(8,128)(2,1)S(1)}, u32[]{:S(2)}, u32[]{:S(2)}) collective-permute-start(bf16[800,512]{1,0:T(8,128)(2,1)S(1)} %get-tuple-element.189), channel_id=1, source_target_pairs={{0,4},{1,3},{2,6},{3,1},{4,0},{5,7},{6,2},{7,5},{8,12},{9,11},{10,... | collective-permute-start | bytes 2457608 | tf_op jit(solution)/shard_map/ppermute | solution.py:608
  82.8 10.8 %collective-permute-start.11 = (bf16[192,512]{1,0:T(8,128)(2,1)S(1)}, bf16[192,512]{1,0:T(8,128)(2,1)S(1)}, u32[]{:S(2)}, u32[]{:S(2)}) collective-permute-start(bf16[192,512]{1,0:T(8,128)(2,1)S(1)} %get-tuple-element.191.refs_0_), channel_id=1, source_target_pairs={{0,16},{1,17},{2,18},{3,19},{4,20},{5,21},{6,22},{7,23},{8,24},{9,... | collective-permute-start | bytes 589832 | tf_op jit(solution)/shard_map/ppermute | solution.py:608
  93.9 8.8 %collective-permute-start.12 = (bf16[416,512]{1,0:T(8,128)(2,1)S(1)}, bf16[416,512]{1,0:T(8,128)(2,1)S(1)}, u32[]{:S(2)}, u32[]{:S(2)}) collective-permute-start(bf16[416,512]{1,0:T(8,128)(2,1)S(1)} %get-tuple-element.195), channel_id=1, source_target_pairs={{0,2},{1,5},{2,0},{3,7},{4,6},{5,1},{6,4},{7,3},{8,10},{9,13},{10,... | collective-permute-start | bytes 1277960 | tf_op jit(solution)/shard_map/ppermute | solution.py:608
  95.4 5.9 %collective-permute-start.13 = (bf16[192,512]{1,0:T(8,128)(2,1)S(1)}, bf16[192,512]{1,0:T(8,128)(2,1)S(1)}, u32[]{:S(2)}, u32[]{:S(2)}) collective-permute-start(bf16[192,512]{1,0:T(8,128)(2,1)S(1)} %get-tuple-element.197.refs_0_), channel_id=1, source_target_pairs={{0,8},{1,9},{2,10},{3,11},{4,12},{5,13},{6,14},{7,15},{8,0},{9,1},... | collective-permute-start | bytes 589832 | tf_op jit(solution)/shard_map/ppermute | solution.py:608
  101.3 7.8 %collective-permute-start.16 = (bf16[384,512]{1,0:T(8,128)(2,1)S(1)}, bf16[384,512]{1,0:T(8,128)(2,1)S(1)}, u32[]{:S(2)}, u32[]{:S(2)}) collective-permute-start(bf16[384,512]{1,0:T(8,128)(2,1)S(1)} %get-tuple-element.207.refs_0_), channel_id=1, source_target_pairs={{0,4},{1,3},{2,6},{3,1},{4,0},{5,7},{6,2},{7,5},{8,12},{9,11},{10,... | collective-permute-start | bytes 1179656 | tf_op jit(solution)/shard_map/ppermute | solution.py:608
  102.8 6.1 %collective-permute-start.14 = (bf16[224,512]{1,0:T(8,128)(2,1)S(1)}, bf16[224,512]{1,0:T(8,128)(2,1)S(1)}, u32[]{:S(2)}, u32[]{:S(2)}) collective-permute-start(bf16[224,512]{1,0:T(8,128)(2,1)S(1)} %get-tuple-element.201), channel_id=1, source_target_pairs={{0,8},{1,9},{2,10},{3,11},{4,12},{5,13},{6,14},{7,15},{8,0},{9,1},... | collective-permute-start | bytes 688136 | tf_op jit(solution)/shard_map/ppermute | solution.py:608
  109.2 12.1 %collective-permute-start.18 = (bf16[768,512]{1,0:T(8,128)(2,1)S(1)}, bf16[768,512]{1,0:T(8,128)(2,1)S(1)}, u32[]{:S(2)}, u32[]{:S(2)}) collective-permute-start(bf16[768,512]{1,0:T(8,128)(2,1)S(1)} %get-tuple-element.211.refs_0_), channel_id=1, source_target_pairs={{0,2},{1,5},{2,0},{3,7},{4,6},{5,1},{6,4},{7,3},{8,10},{9,13},{10,... | collective-permute-start | bytes 2359304 | tf_op jit(solution)/shard_map/ppermute | solution.py:608
  110.8 10.3 %collective-permute-start.15 = (bf16[224,512]{1,0:T(8,128)(2,1)S(1)}, bf16[224,512]{1,0:T(8,128)(2,1)S(1)}, u32[]{:S(2)}, u32[]{:S(2)}) collective-permute-start(bf16[224,512]{1,0:T(8,128)(2,1)S(1)} %get-tuple-element.205), channel_id=1, source_target_pairs={{0,16},{1,17},{2,18},{3,19},{4,20},{5,21},{6,22},{7,23},{8,24},{9,... | collective-permute-start | bytes 688136 | tf_op jit(solution)/shard_map/ppermute | solution.py:608
  121.4 9.0 %collective-permute-start.20 = (bf16[1536,512]{1,0:T(8,128)(2,1)S(1)}, bf16[1536,512]{1,0:T(8,128)(2,1)S(1)}, u32[]{:S(2)}, u32[]{:S(2)}) collective-permute-start(bf16[1536,512]{1,0:T(8,128)(2,1)S(1)} %get-tuple-element.215.refs_0_), channel_id=1, source_target_pairs={{0,1},{1,0},{2,3},{3,2},{4,5},{5,4},{6,7},{7,6},{8,9},{9,8},{10,11... | collective-permute-start | bytes 4718600 | tf_op jit(solution)/shard_map/ppermute | solution.py:608
  121.5 7.3 %collective-permute-start.17 = (bf16[192,512]{1,0:T(8,128)(2,1)S(1)}, bf16[192,512]{1,0:T(8,128)(2,1)S(1)}, u32[]{:S(2)}, u32[]{:S(2)}) collective-permute-start(bf16[192,512]{1,0:T(8,128)(2,1)S(1)} %get-tuple-element.210.refs_0_), channel_id=1, source_target_pairs={{0,8},{1,9},{2,10},{3,11},{4,12},{5,13},{6,14},{7,15},{8,0},{9,1},... | collective-permute-start | bytes 589832 | tf_op jit(solution)/shard_map/ppermute | solution.py:608
  128.8 7.8 %collective-permute-start.19 = (bf16[384,512]{1,0:T(8,128)(2,1)S(1)}, bf16[384,512]{1,0:T(8,128)(2,1)S(1)}, u32[]{:S(2)}, u32[]{:S(2)}) collective-permute-start(bf16[384,512]{1,0:T(8,128)(2,1)S(1)} %get-tuple-element.214.refs_0_), channel_id=1, source_target_pairs={{0,2},{1,5},{2,0},{3,7},{4,6},{5,1},{6,4},{7,3},{8,10},{9,13},{10,... | collective-permute-start | bytes 1179656 | tf_op jit(solution)/shard_map/ppermute | solution.py:608
  136.7 12.4 %collective-permute-start.21 = (bf16[768,512]{1,0:T(8,128)(2,1)S(1)}, bf16[768,512]{1,0:T(8,128)(2,1)S(1)}, u32[]{:S(2)}, u32[]{:S(2)}) collective-permute-start(bf16[768,512]{1,0:T(8,128)(2,1)S(1)} %get-tuple-element.218.refs_0_), channel_id=1, source_target_pairs={{0,4},{1,3},{2,6},{3,1},{4,0},{5,7},{6,2},{7,5},{8,12},{9,11},{10,... | collective-permute-start | bytes 2359304 | tf_op jit(solution)/shard_map/ppermute | solution.py:608
  149.2 3.5 %collective-permute-start.22 = (bf16[1568,512]{1,0:T(8,128)(2,1)S(1)}, bf16[1568,512]{1,0:T(8,128)(2,1)S(1)}, u32[]{:S(2)}, u32[]{:S(2)}) collective-permute-start(bf16[1568,512]{1,0:T(8,128)(2,1)S(1)} %get-tuple-element.221.refs_0_.refs_7_), channel_id=1, source_target_pairs={{0,1},{1,0},{2,3},{3,2},{4,5},{5,4},{6,7},{7,6},{8,9},{9,8},{10,11... | collective-permute-start | bytes 4816904 | tf_op jit(solution)/shard_map/ppermute | solution.py:608
